TPU v7x, 32 devices: a whole 2x2x4 slice. The times are simulated.
32 devices in a mesh: pairs: 16 (over z, y, x), aux: 2 (over core).
Axes of the slice: x: 2, y: 2, z: 4, core: 2. Of those that a mesh axis runs over, the one named last changes fastest.
Arguments:
- densities: bfloat16 [16, 12288], P(None, 'pairs'), may hold values from -6 to 6
- tensor: bfloat16 [12288, 20480], P('pairs', 'aux'), may hold values from -0.078125 to 0.078125
- metric: bfloat16 [20480, 20480], P('aux', 'pairs'), may hold values from -0.0390625 to 0.0390625
- row_count: int32 [16], P('pairs'), may hold values from 1 to 768, 7680 in all
Outputs:
- coulomb: bfloat16 [16, 12288], P('aux', 'pairs')
Inputs may be any that keep to these rules, and one draw needn't show every extreme that they name: The first row_count[b] rows of pair block b are live; some block has all 768 rows live.
All inputs are finite; a program needn't handle non-finite values.
Results may differ from a plain program's by a relative error of at most 0.0057.
Values may be sent and summed in bfloat16 or wider, within the bound.
No kernel may reach another device: no remote copies, remote signals or barrier semaphores. Data moves between devices by JAX's collectives and lax.ppermute only.
A program may use at most 128 MiB of HBM per device.

v0:
```python
import jax
import jax.numpy as jnp
from jax import lax
from jax.sharding import PartitionSpec as P


def body(densities, tensor, metric, row_count):
    rows_here = tensor.shape[0]
    half_aux = tensor.shape[1]
    live = lax.broadcasted_iota(jnp.int32, (1, rows_here), 1) < row_count[0]
    masked = jnp.where(live, densities, jnp.zeros_like(densities))
    fit_part = jnp.dot(masked, tensor, preferred_element_type=jnp.float32)
    fitted = lax.psum(fit_part, "pairs").astype(jnp.bfloat16)
    solved_part = jnp.dot(fitted, metric, preferred_element_type=jnp.float32)
    summed = lax.psum(solved_part, "aux").astype(jnp.bfloat16)
    solved = lax.all_gather(summed, "pairs", axis=1, tiled=True)
    own_block = lax.dynamic_slice_in_dim(solved, lax.axis_index("aux") * half_aux, half_aux, 1)
    back_term = lax.dot_general(
        own_block, tensor, (((1,), (1,)), ((), ())), preferred_element_type=jnp.float32
    )
    returned = lax.psum_scatter(back_term, "aux", scatter_dimension=0, tiled=True)
    return jnp.where(live, returned, jnp.zeros_like(returned)).astype(jnp.bfloat16)


def solution(mesh):
    placed = (P(None, "pairs"), P("pairs", "aux"), P("aux", "pairs"), P("pairs"))
    return jax.shard_map(
        body, mesh=mesh, in_specs=placed, out_specs=P("aux", "pairs"), check_vma=False
    )
```

profile of v0, /device:TPU:0, one launch (start us, length us, event | category | flops | bytes accessed | tf_op | source)
XLA Modules:
  0.0 178.0 jit_solution(6815212649878766157)
XLA Ops:
  6.5 0.0 reduce-scatter.2.cloned.1.call-start
  7.2 7.6 %fusion.4 = f32[16,10240]{1,0:T(8,128)S(1)} fusion(bf16[768,10240]{1,0:T(8,128)(2,1)} %param.5, bf16[16,768]{1,0:T(8,128)(2,1)} %param.4, pred[768]{0:T(1024)(128)(4,1)S(1)} %iota_compare_fusion), kind=kOutput, calls=%fused_computation.5 | convolution fusion | flops 251670528 | bytes 16409344 | tf_op jit(solution)/shard_map/dot_general | solution.py:12
  14.8 86.2 %all-reduce.1 = bf16[16,10240]{1,0:T(8,128)(2,1)S(1)} all-reduce(f32[16,10240]{1,0:T(8,128)S(1)} %fusion.4), channel_id=1, replica_groups=mesh['pairs'=16,'aux'=2] {'pairs'}, use_global_device_ids=true, to_apply=%region_0.1 | all-reduce | flops 163840 | bytes 983040 | tf_op jit(solution)/shard_map/psum | solution.py:13
  101.1 10.3 %fusion.10 = f32[16,1280]{1,0:T(8,128)S(1)} fusion(bf16[16,10240]{1,0:T(8,128)(2,1)S(1)} %all-reduce.1, bf16[10240,1280]{1,0:T(8,128)(2,1)} %param.6), kind=kOutput, calls=%fused_computation.12 | convolution fusion | flops 419430400 | bytes 26624000 | tf_op jit(solution)/shard_map/dot_general | solution.py:14
  111.4 3.6 %psum.15 = bf16[16,1280]{1,0:T(8,128)(2,1)S(1)} all-reduce(f32[16,1280]{1,0:T(8,128)S(1)} %fusion.10), channel_id=1, replica_groups=mesh['pairs'=16,'aux'=2] {'aux'}, use_global_device_ids=true, to_apply=%region_1.2 | all-reduce | flops 20480 | bytes 122880 | tf_op jit(solution)/shard_map/psum | solution.py:15
  115.0 39.1 %all_gather.3 = bf16[16,20480]{1,0:T(8,128)(2,1)S(1)} all-gather(bf16[16,1280]{1,0:T(8,128)(2,1)S(1)} %psum.15), channel_id=1, replica_groups=mesh['pairs'=16,'aux'=2] {'pairs'}, dimensions={1}, use_global_device_ids=true | all-gather | bytes 696320 | tf_op jit(solution)/shard_map/all_gather | solution.py:16
  154.1 10.3 %fusion = f32[16,768]{1,0:T(8,128)} fusion(bf16[768,10240]{1,0:T(8,128)(2,1)} %param.5, bf16[16,20480]{1,0:T(8,128)(2,1)S(1)} %all_gather.3, s32[]{:T(128)S(6)} %select_n.12), kind=kOutput, calls=%fused_computation | convolution fusion | flops 251658240 | bytes 16105476 | tf_op jit(solution)/shard_map/dot_general | solution.py:18
  164.3 0.0 reduce-scatter.2.cloned.1.call-update
  164.3 5.4 %reduce-scatter.2.cloned.1.call-done = f32[8,768]{1,0:T(8,128)} async-done(((f32[16,768]{1,0:T(8,128)}), f32[8,768]{1,0:T(8,128)}) %reduce-scatter.2.cloned.1.call-update) | async-done | bytes 24592 | tf_op jit(solution)/shard_map/reduce_scatter | solution.py:21
  169.8 1.3 select_convert_fusion
  (1 shorter events, 0.0 us)
Async XLA Ops:
  6.5 163.3 %reduce-scatter.2.cloned.1.call-start = ((), (), s32[]{:S(2)}) async-start(), calls=%async_computation.1 | async-start | bytes 73728 | tf_op jit(solution)/shard_map/reduce_scatter | solution.py:21
Sparse Core Ops, SparseCore 0:
  164.5 5.2 reduce-scatter.1
where the time goes:
time: 178 us
  blocking collectives  129 us (72%)
  matrix products  28.2 us (16%)
  between operations  14.1 us (8%)
  waiting for transfers between devices  5.46 us (3%)
    psum x1, blocking collectives, body(): fitted = lax.psum(fit_part, 'pairs').astype(jnp.bfloat16)  86.2 us
    all_gather x1, blocking collectives, body(): solved = lax.all_gather(summed, 'pairs', axis=1, tiled=True)  39.1 us
    dot_general x1, matrix products, body(): lax.dot_general(own_block, tensor, (((1,), (1,)), ((), ())), preferred_el...  10.3 us
    dot_general x1, matrix products, body(): solved_part = jnp.dot(fitted, metric, preferred_element_type=jnp.float32)  10.3 us
    dot_general x1, matrix products, body(): fit_part = jnp.dot(masked, tensor, preferred_element_type=jnp.float32)  7.64 us
    reduce_scatter x1, waiting for transfers between devices, body(): lax.psum_scatter(back_term, 'aux', scatter_dimension=0, tiled=True)  5.44 us
    psum x1, blocking collectives, body(): summed = lax.psum(solved_part, 'aux').astype(jnp.bfloat16)  3.64 us
  transfers between devices with their start and end apart: 1, of which 1 were waited for; matrix products, arithmetic and copies ran while one was open for 0% of the time, Pallas kernels for 0%

commit v1 on v0

v1 whole, which is shorter than its diff:
```python
import functools

import jax
import jax.numpy as jnp
from jax import lax
from jax.experimental import pallas as pl
from jax.experimental.pallas import tpu as pltpu
from jax.sharding import PartitionSpec as P

F32, BF16 = jnp.float32, jnp.bfloat16
MIB = 1 << 20


def digits_of(count):
    sizes = []
    while count > 1:
        size = 4 if count % 4 == 0 else 2
        sizes.append(size)
        count //= size
    return sizes


def largest_step(extent, limit, unit):
    return max(s for s in range(unit, limit + 1, unit) if extent % s == 0)


def swap(x, axis, count, mask):
    return lax.ppermute(x, axis, [(i, i ^ mask) for i in range(count)])


def params(used_bytes):
    return pltpu.CompilerParams(vmem_limit_bytes=used_bytes + 4 * MIB)


def fit_kernel(picks, step, digit_ref, count_ref, dens_ref, tensor_ref, *rest):
    outs, (held, sems) = rest[: len(picks)], rest[len(picks) :]
    width = outs[0].shape[1]
    copies = []
    for at, pick in enumerate(picks):
        first = (digit_ref[0] ^ pick) * width
        for j in range(width // step):
            slot = at * (width // step) + j
            copy = pltpu.make_async_copy(
                tensor_ref.at[:, pl.ds(pl.multiple_of(first + j * step, 128), step)],
                held.at[slot],
                sems.at[slot],
            )
            copy.start()
            copies.append(copy)
    dens = dens_ref[...]
    live = lax.broadcasted_iota(jnp.int32, dens.shape, 1) < count_ref[0]
    masked = jnp.where(live, dens.astype(F32), 0.0).astype(BF16)
    for at in range(len(picks)):
        for j in range(width // step):
            slot = at * (width // step) + j
            copies[slot].wait()
            term = jnp.dot(masked, held[slot], preferred_element_type=F32)
            outs[at][:, j * step : (j + 1) * step] = term.astype(outs[at].dtype)


def fit(picks, dtype, width, digit, row_count, densities, tensor):
    rows = tensor.shape[0]
    step = largest_step(width, 512, 128)
    slots = len(picks) * width // step
    smem = pl.BlockSpec(memory_space=pltpu.SMEM)
    vmem = pl.BlockSpec(memory_space=pltpu.VMEM)
    return pl.pallas_call(
        functools.partial(fit_kernel, picks, step),
        out_shape=[jax.ShapeDtypeStruct((densities.shape[0], width), dtype) for _ in picks],
        in_specs=[smem, smem, vmem, pl.BlockSpec(memory_space=pltpu.HBM)],
        out_specs=[vmem for _ in picks],
        scratch_shapes=[
            pltpu.VMEM((slots, rows, step), BF16),
            pltpu.SemaphoreType.DMA((slots,)),
        ],
        compiler_params=params(slots * rows * step * 2),
        cost_estimate=pl.CostEstimate(
            flops=2 * 16 * rows * step * slots,
            bytes_accessed=slots * rows * step * 2,
            transcendentals=0,
        ),
    )(digit, row_count, densities, pltpu.with_memory_space_constraint(tensor, pltpu.HBM))


def solve_kernel(picks, step, begun, digit_ref, metric_ref, *rest):
    fitted, rest = rest[: len(picks)], rest[len(picks) :]
    if begun:
        start_ref, rest = rest[0], rest[1:]
    out_ref, held, sems = rest
    depth = fitted[0].shape[1]
    copies = []
    for at, pick in enumerate(picks):
        first = (digit_ref[0] ^ pick) * depth
        for j in range(depth // step):
            slot = at * (depth // step) + j
            copy = pltpu.make_async_copy(
                metric_ref.at[pl.ds(pl.multiple_of(first + j * step, 128), step), :],
                held.at[slot],
                sems.at[slot],
            )
            copy.start()
            copies.append(copy)
    total = start_ref[...] if begun else jnp.zeros(out_ref.shape, F32)
    for at in range(len(picks)):
        for j in range(depth // step):
            slot = at * (depth // step) + j
            copies[slot].wait()
            total += jnp.dot(
                fitted[at][:, j * step : (j + 1) * step], held[slot], preferred_element_type=F32
            )
    out_ref[...] = total


def solve(picks, digit, metric, fitted, begun=None):
    depth, width = fitted[0].shape[1], metric.shape[1]
    step = largest_step(depth, 512, 128)
    slots = len(picks) * depth // step
    smem = pl.BlockSpec(memory_space=pltpu.SMEM)
    vmem = pl.BlockSpec(memory_space=pltpu.VMEM)
    extra = [] if begun is None else [begun]
    return pl.pallas_call(
        functools.partial(solve_kernel, picks, step, begun is not None),
        out_shape=jax.ShapeDtypeStruct((fitted[0].shape[0], width), F32),
        in_specs=[smem, pl.BlockSpec(memory_space=pltpu.HBM)] + [vmem] * (len(picks) + len(extra)),
        out_specs=vmem,
        scratch_shapes=[
            pltpu.VMEM((slots, step, width), BF16),
            pltpu.SemaphoreType.DMA((slots,)),
        ],
        compiler_params=params(slots * step * width * 2),
        cost_estimate=pl.CostEstimate(
            flops=2 * 16 * width * step * slots,
            bytes_accessed=slots * step * width * 2,
            transcendentals=0,
        ),
    )(digit, pltpu.with_memory_space_constraint(metric, pltpu.HBM), *fitted, *extra)


def back_kernel(step, begun, starts_ref, tensor_ref, pieces_ref, *rest):
    if begun:
        start_ref, rest = rest[0], rest[1:]
    out_ref, held, sems = rest
    count, _, width = pieces_ref.shape
    per = width // step
    copies = []
    for i in range(count):
        for j in range(per):
            copy = pltpu.make_async_copy(
                tensor_ref.at[:, pl.ds(pl.multiple_of(starts_ref[i] + j * step, 128), step)],
                held.at[i * per + j],
                sems.at[i * per + j],
            )
            copy.start()
            copies.append(copy)
    total = start_ref[...] if begun else jnp.zeros(out_ref.shape, F32)
    for i in range(count):
        for j in range(per):
            copies[i * per + j].wait()
            total += lax.dot_general(
                pieces_ref[i, :, j * step : (j + 1) * step],
                held[i * per + j],
                (((1,), (1,)), ((), ())),
                preferred_element_type=F32,
            )
    out_ref[...] = total


def back(starts, tensor, pieces, begun=None):
    rows = tensor.shape[0]
    count, k, width = pieces.shape
    step = largest_step(width, 640, 128)
    slots = count * width // step
    smem = pl.BlockSpec(memory_space=pltpu.SMEM)
    vmem = pl.BlockSpec(memory_space=pltpu.VMEM)
    extra = [] if begun is None else [begun]
    return pl.pallas_call(
        functools.partial(back_kernel, step, begun is not None),
        out_shape=jax.ShapeDtypeStruct((k, rows), F32),
        in_specs=[smem, pl.BlockSpec(memory_space=pltpu.HBM), vmem] + [vmem] * len(extra),
        out_specs=vmem,
        scratch_shapes=[
            pltpu.VMEM((slots, rows, step), BF16),
            pltpu.SemaphoreType.DMA((slots,)),
        ],
        compiler_params=params(slots * rows * step * 2),
        cost_estimate=pl.CostEstimate(
            flops=2 * 16 * rows * step * slots,
            bytes_accessed=slots * rows * step * 2,
            transcendentals=0,
        ),
    )(starts, pltpu.with_memory_space_constraint(tensor, pltpu.HBM), pieces, *extra)


def body(n_pairs, densities, tensor, metric, row_count):
    rows, half_aux = tensor.shape
    block = metric.shape[1]
    sizes = digits_of(n_pairs)
    me = lax.axis_index("pairs")
    core = lax.axis_index("aux")
    first, rest = sizes[0], sizes[1:]
    digit = (me % first).astype(jnp.int32).reshape(1)
    width = half_aux // first

    others = list(range(first - 1, 0, -1))
    sent = fit(others, BF16, width, digit, row_count, densities, tensor)
    arrived = [swap(x, "pairs", n_pairs, pick) for x, pick in zip(sent, others)]
    (total,) = fit([0], F32, width, digit, row_count, densities, tensor)
    for x in arrived:
        total = total + x.astype(F32)
    stride = first
    for size in rest:
        sending = total.astype(BF16)
        arrived = [swap(sending, "pairs", n_pairs, pick * stride) for pick in range(1, size)]
        for x in arrived:
            total = total + x.astype(F32)
        stride *= size
    fitted = total.astype(BF16)

    gathered = [swap(fitted, "pairs", n_pairs, pick) for pick in others]
    part = solve([0], digit, metric, [fitted])
    part = solve(others, digit, metric, gathered, part)

    half = block // 2
    keep = lax.dynamic_slice_in_dim(part, core * half, half, 1)
    give = lax.dynamic_slice_in_dim(part, (1 - core) * half, half, 1)
    piece = (keep + swap(give, "aux", 2, 1)).astype(BF16)

    last = sizes[-1]
    low = n_pairs // last
    mine = me // low
    got = []
    for pick in range(last):
        pairs = []
        for line in range(low):
            for high in range(last):
                a, i = high // (last // 2), high % (last // 2)
                for c in range(2):
                    to = (2 * i + c) ^ pick
                    pairs.append(((high * low + line) * 2 + c, (to * low + line) * 2 + a))
        got.append(lax.ppermute(piece, ("pairs", "aux"), pairs))
    held = jnp.stack(got)
    order = [mine ^ pick for pick in range(last)]
    origin = jnp.stack([(o // 2) * low * block + (o % 2) * half for o in order])

    line = me % low
    pieces, starts = held, origin + line * block
    if half % 128 == 0 and len(sizes) == 2:
        arrived = [swap(held, "pairs", n_pairs, pick) for pick in others]
        begun = back(starts.astype(jnp.int32), tensor, held)
        pieces = jnp.concatenate(arrived)
        starts = jnp.concatenate([origin + (line ^ pick) * block for pick in others])
        returned = back(starts.astype(jnp.int32), tensor, pieces, begun)
    else:
        stride = 1
        lines = [line]
        pieces = held[None]
        for size in sizes[:-1]:
            arrived = [pieces] + [swap(pieces, "pairs", n_pairs, pick * stride) for pick in range(1, size)]
            lines = [x ^ (pick * stride) for pick in range(size) for x in lines]
            pieces = jnp.concatenate(arrived)
            stride *= size
        whole = jnp.zeros((densities.shape[0], half_aux), BF16)
        for at, x in enumerate(lines):
            for pick in range(last):
                whole = lax.dynamic_update_slice_in_dim(
                    whole, pieces[at, pick], origin[pick] + x * block, 1
                )
        step = largest_step(half_aux, 640, 128)
        count = half_aux // step
        pieces = whole.reshape(-1, count, step).transpose(1, 0, 2)
        returned = back(jnp.arange(count, dtype=jnp.int32) * step, tensor, pieces)

    k_half = densities.shape[0] // 2
    keep = lax.dynamic_slice_in_dim(returned, core * k_half, k_half, 0)
    give = lax.dynamic_slice_in_dim(returned, (1 - core) * k_half, k_half, 0)
    coulomb = keep + swap(give, "aux", 2, 1)
    live = lax.broadcasted_iota(jnp.int32, (1, rows), 1) < row_count[0]
    return jnp.where(live, coulomb, 0.0).astype(BF16)


def solution(mesh):
    placed = (P(None, "pairs"), P("pairs", "aux"), P("aux", "pairs"), P("pairs"))
    return jax.shard_map(
        functools.partial(body, mesh.shape["pairs"]),
        mesh=mesh,
        in_specs=placed,
        out_specs=P("aux", "pairs"),
        check_vma=False,
    )
```

time: 178 us -> 67.2 us (0.38)
  blocking collectives: 129 us -> 0 us
  matrix products: 28.2 us -> 0 us
  Pallas kernels: 0 us -> 27.9 us
  starting transfers between devices: 0.01 us -> 24.8 us
  between operations: 14.1 us -> 0.85 us
  waiting for transfers between devices: 5.46 us -> 11.6 us
    psum x2 -> x0, blocking collectives: 89.9 us -> none  [the longest x1 86.2 us: body(): fitted = lax.psum(fit_part, 'pairs').astype(jnp.bfloat16)]
    all_gather x1 -> x0, blocking collectives: 39.1 us -> none  [body(): solved = lax.all_gather(summed, 'pairs', axis=1, tiled=True)]
    dot_general x3 -> x0, matrix products: 28.2 us -> none  [the longest x1 10.3 us: body(): lax.dot_general(own_block, tensor, (((1,), (1,)), ((), ())), preferred_el...]
    pallas_call x0 -> x6, Pallas kernels: none -> 27.9 us  [the longest x2 10.4 us: back(): pl.pallas_call(functools.partial(back_kernel, step, begun is not None), o...]
    ppermute x0 -> x18, starting transfers between devices: none -> 24.8 us  [the longest x14 17.9 us: swap(): return lax.ppermute(x, axis, [(i, i ^ mask) for i in range(count)])]
    ppermute x0 -> x18, waiting for transfers between devices: none -> 11.6 us  [the longest x14 10.5 us: swap(): return lax.ppermute(x, axis, [(i, i ^ mask) for i in range(count)])]
    reduce_scatter x1 -> x0, waiting for transfers between devices: 5.44 us -> none  [body(): lax.psum_scatter(back_term, 'aux', scatter_dimension=0, tiled=True)]
  transfers between devices with their start and end apart: 1 -> 18, of which waited for: 1 -> 9; matrix products, arithmetic and copies ran while one was open for 0% -> 0% of each run, Pallas kernels for 0% -> 14%
where the time goes in v1:
time: 67.2 us; the launch traced here: 66.8 us
  Pallas kernels  27.9 us (42%)
  starting transfers between devices  24.8 us (37%)
  waiting for transfers between devices  11.6 us (17%)
  other arithmetic  0.95 us (1%)
  between operations  0.85 us (1%)
  local copies, waits for them, and re-layouts  0.76 us (1%)
    ppermute x14, starting transfers between devices, swap(): return lax.ppermute(x, axis, [(i, i ^ mask) for i in range(count)])  17.9 us
    ppermute x14, waiting for transfers between devices, swap(): return lax.ppermute(x, axis, [(i, i ^ mask) for i in range(count)])  10.5 us
    pallas_call x2, Pallas kernels, back(): pl.pallas_call(functools.partial(back_kernel, step, begun is not None), o...  10.4 us
    pallas_call x2, Pallas kernels, solve(): pl.pallas_call(functools.partial(solve_kernel, picks, step, begun is not...  10.3 us
    pallas_call x2, Pallas kernels, fit(): pl.pallas_call(functools.partial(fit_kernel, picks, step), out_shape=[jax...  7.16 us
    ppermute x4, starting transfers between devices, body(): got.append(lax.ppermute(piece, ('pairs', 'aux'), pairs))  6.89 us
  transfers between devices with their start and end apart: 18, of which 9 were waited for; matrix products, arithmetic and copies ran while one was open for 0% of the time, Pallas kernels for 14%

profile of v1, /device:TPU:0, one launch (start us, length us, event | category | flops | bytes accessed | tf_op | source)
XLA Modules:
  0.0 66.8 jit_solution(3757329257962282375)
XLA Ops:
  0.7 0.0 copy-start
  0.7 0.7 %copy-done = bf16[16,768]{1,0:T(8,128)(2,1)S(1)} copy-done((bf16[16,768]{1,0:T(8,128)(2,1)S(1)}, bf16[16,768]{1,0:T(8,128)(2,1)}, u32[]{:S(2)}) %copy-start) | copy-done | bytes 24600
  1.4 4.8 %shard_map.47 = (bf16[16,2560]{1,0:T(8,128)(2,1)S(1)}, bf16[16,2560]{1,0:T(8,128)(2,1)S(1)}, bf16[16,2560]{1,0:T(8,128)(2,1)S(1)}) custom-call(s32[1]{0:T(128)} %bitcast.5.digit_ref, s32[1]{0:T(128)} %copy.5.count_ref, bf16[16,768]{1,0:T(8,128)(2,1)S(1)} %copy-done, bf16[768,10240]{1,0:T(8,128)(2,1)} %tensor_ref.7), custom_call_target="tpu_custom_call" | custom-call | flops 188743680 | bytes 11796480 | tf_op jit(solution)/shard_map/pallas_call | solution.py:67
  6.2 3.0 %collective-permute-start.2 = (bf16[16,2560]{1,0:T(8,128)(2,1)S(1)}, bf16[16,2560]{1,0:T(8,128)(2,1)S(1)}, u32[]{:S(2)}, u32[]{:S(2)}) collective-permute-start(bf16[16,2560]{1,0:T(8,128)(2,1)S(1)} %get-tuple-element.10), channel_id=1, source_target_pairs={{0,2},{2,0},{4,6},{6,4},{8,10},{10,8},{12,14},{14,12},{16,18},{18,... | collective-permute-start | bytes 245768 | tf_op jit(solution)/shard_map/ppermute | solution.py:28
  9.2 1.5 %collective-permute-start.1 = (bf16[16,2560]{1,0:T(8,128)(2,1)S(1)}, bf16[16,2560]{1,0:T(8,128)(2,1)S(1)}, u32[]{:S(2)}, u32[]{:S(2)}) collective-permute-start(bf16[16,2560]{1,0:T(8,128)(2,1)S(1)} %get-tuple-element.9), channel_id=1, source_target_pairs={{0,4},{2,6},{4,0},{6,2},{8,12},{10,14},{12,8},{14,10},{16,20},{18,... | collective-permute-start | bytes 245768 | tf_op jit(solution)/shard_map/ppermute | solution.py:28
  10.7 0.0 collective-permute-start
  10.7 2.4 %shard_map.46 = f32[16,2560]{1,0:T(8,128)S(1)} custom-call(s32[1]{0:T(128)} %bitcast.5.digit_ref, s32[1]{0:T(128)} %copy.5.count_ref, bf16[16,768]{1,0:T(8,128)(2,1)S(1)} %copy-done, bf16[768,10240]{1,0:T(8,128)(2,1)} %tensor_ref.7), custom_call_target="tpu_custom_call" | custom-call | flops 62914560 | bytes 3932160 | tf_op jit(solution)/shard_map/pallas_call | solution.py:67
  13.1 0.0 collective-permute-done.2
  13.1 1.4 %collective-permute-done.1 = bf16[16,2560]{1,0:T(8,128)(2,1)S(1)} collective-permute-done((bf16[16,2560]{1,0:T(8,128)(2,1)S(1)}, bf16[16,2560]{1,0:T(8,128)(2,1)S(1)}, u32[]{:S(2)}, u32[]{:S(2)}) %collective-permute-start.1) | collective-permute-done | bytes 81952 | tf_op jit(solution)/shard_map/ppermute | solution.py:28
  14.5 1.5 %collective-permute-done = bf16[16,2560]{1,0:T(8,128)(2,1)S(1)} collective-permute-done((bf16[16,2560]{1,0:T(8,128)(2,1)S(1)}, bf16[16,2560]{1,0:T(8,128)(2,1)S(1)}, u32[]{:S(2)}, u32[]{:S(2)}) %collective-permute-start) | collective-permute-done | bytes 81952 | tf_op jit(solution)/shard_map/ppermute | solution.py:28
  16.1 3.7 %collective-permute-start.5 = (bf16[16,2560]{1,0:T(8,128)(2,1)S(1)}, bf16[16,2560]{1,0:T(8,128)(2,1)S(1)}, u32[]{:S(2)}, u32[]{:S(2)}) collective-permute-start(bf16[16,2560]{1,0:T(8,128)(2,1)S(1)} %fusion), channel_id=1, source_target_pairs={{0,24},{2,26},{4,28},{6,30},{8,16},{10,18},{12,20},{14,22},{16,8},... | collective-permute-start | bytes 245768 | tf_op jit(solution)/shard_map/ppermute | solution.py:28
  19.8 0.0 collective-permute-start.4
  19.8 0.8 %collective-permute-start.3 = (bf16[16,2560]{1,0:T(8,128)(2,1)S(1)}, bf16[16,2560]{1,0:T(8,128)(2,1)S(1)}, u32[]{:S(2)}, u32[]{:S(2)}) collective-permute-start(bf16[16,2560]{1,0:T(8,128)(2,1)S(1)} %fusion), channel_id=1, source_target_pairs={{0,8},{2,10},{4,12},{6,14},{8,0},{10,2},{12,4},{14,6},{16,24},{18,... | collective-permute-start | bytes 245768 | tf_op jit(solution)/shard_map/ppermute | solution.py:28
  20.6 1.9 %collective-permute-done.5 = bf16[16,2560]{1,0:T(8,128)(2,1)S(1)} collective-permute-done((bf16[16,2560]{1,0:T(8,128)(2,1)S(1)}, bf16[16,2560]{1,0:T(8,128)(2,1)S(1)}, u32[]{:S(2)}, u32[]{:S(2)}) %collective-permute-start.5) | collective-permute-done | bytes 81952 | tf_op jit(solution)/shard_map/ppermute | solution.py:28
  22.5 3.0 %collective-permute-done.4 = bf16[16,2560]{1,0:T(8,128)(2,1)S(1)} collective-permute-done((bf16[16,2560]{1,0:T(8,128)(2,1)S(1)}, bf16[16,2560]{1,0:T(8,128)(2,1)S(1)}, u32[]{:S(2)}, u32[]{:S(2)}) %collective-permute-start.4) | collective-permute-done | bytes 81952 | tf_op jit(solution)/shard_map/ppermute | solution.py:28
  25.5 0.0 collective-permute-done.3
  25.5 0.1 add_convert_fusion.rest_0_
  25.6 1.1 %collective-permute-start.6 = (bf16[16,2560]{1,0:T(8,128)(2,1)S(1)}, bf16[16,2560]{1,0:T(8,128)(2,1)S(1)}, u32[]{:S(2)}, u32[]{:S(2)}) collective-permute-start(bf16[16,2560]{1,0:T(8,128)(2,1)S(1)} %add_convert_fusion.rest_0_), channel_id=1, source_target_pairs={{0,6},{2,4},{4,2},{6,0},{8,14},{10,12},{12,10},{14,8},{16,22},{18,... | collective-permute-start | bytes 245768 | tf_op jit(solution)/shard_map/ppermute | solution.py:28
  26.7 1.4 %collective-permute-start.7 = (bf16[16,2560]{1,0:T(8,128)(2,1)S(1)}, bf16[16,2560]{1,0:T(8,128)(2,1)S(1)}, u32[]{:S(2)}, u32[]{:S(2)}) collective-permute-start(bf16[16,2560]{1,0:T(8,128)(2,1)S(1)} %add_convert_fusion.rest_0_), channel_id=1, source_target_pairs={{0,4},{2,6},{4,0},{6,2},{8,12},{10,14},{12,8},{14,10},{16,20},{18,... | collective-permute-start | bytes 245768 | tf_op jit(solution)/shard_map/ppermute | solution.py:28
  28.1 1.0 %collective-permute-start.8 = (bf16[16,2560]{1,0:T(8,128)(2,1)S(1)}, bf16[16,2560]{1,0:T(8,128)(2,1)S(1)}, u32[]{:S(2)}, u32[]{:S(2)}) collective-permute-start(bf16[16,2560]{1,0:T(8,128)(2,1)S(1)} %add_convert_fusion.rest_0_), channel_id=1, source_target_pairs={{0,2},{2,0},{4,6},{6,4},{8,10},{10,8},{12,14},{14,12},{16,18},{18,... | collective-permute-start | bytes 245768 | tf_op jit(solution)/shard_map/ppermute | solution.py:28
  29.1 3.3 %shard_map.48.rest_3_ = f32[16,1280]{1,0:T(8,128)S(1)} custom-call(s32[1]{0:T(128)} %bitcast.5.digit_ref, bf16[10240,1280]{1,0:T(8,128)(2,1)} %metric_ref.3, bf16[16,2560]{1,0:T(8,128)(2,1)S(1)} %add_convert_fusion.rest_0_), custom_call_target="tpu_custom_call" | custom-call | flops 104857600 | bytes 6553600 | tf_op jit(solution)/shard_map/pallas_call | solution.py:121
  32.4 0.0 collective-permute-done.6.rest_0_
  32.4 0.0 collective-permute-done.7.rest_1_
  32.4 0.1 collective-permute-done.8.rest_2_
  32.5 7.1 %shard_map.49 = f32[16,1280]{1,0:T(8,128)S(1)} custom-call(s32[1]{0:T(128)} %bitcast.5.digit_ref, bf16[10240,1280]{1,0:T(8,128)(2,1)} %metric_ref.3, bf16[16,2560]{1,0:T(8,128)(2,1)S(1)} %collective-permute-done.6.rest_0_, bf16[16,2560]{1,0:T(8,128)(2,1)S(1)} %collective-permute-done.7.rest_1_, bf16[16,2560]{1,0:T(8,128)(2,1)S(1)} %collective-permute-done.8.rest_2_, ...), custom_call_target="tpu_custom_call" | custom-call | flops 314572800 | bytes 19660800 | tf_op jit(solution)/shard_map/pallas_call | solution.py:121
  39.6 0.1 collective-permute-start.9
  39.7 0.1 broadcast_add_fusion
  39.8 1.1 %collective-permute-done.9 = f32[16,640]{1,0:T(8,128)S(1)} collective-permute-done((f32[16,640]{1,0:T(8,128)S(1)}, f32[16,640]{1,0:T(8,128)S(1)}, u32[]{:S(2)}, u32[]{:S(2)}) %collective-permute-start.9) | collective-permute-done | bytes 40992 | tf_op jit(solution)/shard_map/ppermute | solution.py:28
  40.9 4.2 %collective-permute-start.13 = (bf16[16,640]{1,0:T(8,128)(2,1)S(1)}, bf16[16,640]{1,0:T(8,128)(2,1)S(1)}, u32[]{:S(2)}, u32[]{:S(2)}) collective-permute-start(bf16[16,640]{1,0:T(8,128)(2,1)S(1)} %add_convert_fusion.1), channel_id=1, source_target_pairs={{0,24},{1,16},{8,8},{9,0},{16,25},{17,17},{24,9},{25,1},{2,26},{3,... | collective-permute-start | bytes 61448 | tf_op jit(solution)/shard_map/ppermute | solution.py:240
  45.1 0.4 collective-permute-start.12
  45.5 1.7 %collective-permute-start.11 = (bf16[16,640]{1,0:T(8,128)(2,1)S(1)}, bf16[16,640]{1,0:T(8,128)(2,1)S(1)}, u32[]{:S(2)}, u32[]{:S(2)}) collective-permute-start(bf16[16,640]{1,0:T(8,128)(2,1)S(1)} %add_convert_fusion.1), channel_id=1, source_target_pairs={{0,8},{1,0},{8,24},{9,16},{16,9},{17,1},{24,25},{25,17},{2,10},{3,... | collective-permute-start | bytes 61448 | tf_op jit(solution)/shard_map/ppermute | solution.py:240
  47.2 0.7 collective-permute-start.10
  47.9 0.0 collective-permute-done.13
  47.9 1.1 %collective-permute-done.12 = bf16[16,640]{1,0:T(8,128)(2,1)S(1)} collective-permute-done((bf16[16,640]{1,0:T(8,128)(2,1)S(1)}, bf16[16,640]{1,0:T(8,128)(2,1)S(1)}, u32[]{:S(2)}, u32[]{:S(2)}) %collective-permute-start.12) | collective-permute-done | bytes 20512 | tf_op jit(solution)/shard_map/ppermute | solution.py:240
  48.9 0.0 collective-permute-done.11
  48.9 0.0 collective-permute-done.10
  49.0 1.1 %collective-permute-start.16 = (bf16[4,16,640]{2,1,0:T(8,128)(2,1)S(1)}, bf16[4,16,640]{2,1,0:T(8,128)(2,1)S(1)}, u32[]{:S(2)}, u32[]{:S(2)}) collective-permute-start(bf16[4,16,640]{2,1,0:T(8,128)(2,1)S(1)} %pad_maximum_fusion.1.pieces_ref), channel_id=1, source_target_pairs={{0,2},{2,0},{4,6},{6,4},{8,10},{10,8},{12,14},{14,12},{16,18},{18,... | collective-permute-start | bytes 245768 | tf_op jit(solution)/shard_map/ppermute | solution.py:28
  50.1 0.7 collective-permute-start.15
  50.7 1.8 %collective-permute-start.14 = (bf16[4,16,640]{2,1,0:T(8,128)(2,1)S(1)}, bf16[4,16,640]{2,1,0:T(8,128)(2,1)S(1)}, u32[]{:S(2)}, u32[]{:S(2)}) collective-permute-start(bf16[4,16,640]{2,1,0:T(8,128)(2,1)S(1)} %pad_maximum_fusion.1.pieces_ref), channel_id=1, source_target_pairs={{0,6},{2,4},{4,2},{6,0},{8,14},{10,12},{12,10},{14,8},{16,22},{18,... | collective-permute-start | bytes 245768 | tf_op jit(solution)/shard_map/ppermute | solution.py:28
  52.5 0.1 pad_add_fusion.1.starts_ref
  52.6 3.6 %shard_map.50.rest_0_ = f32[16,768]{1,0:T(8,128)S(1)} custom-call(s32[4]{0:T(128)S(1)} %get-tuple-element.11.starts_ref, bf16[768,10240]{1,0:T(8,128)(2,1)} %tensor_ref.7, bf16[4,16,640]{2,1,0:T(8,128)(2,1)S(1)} %pad_maximum_fusion.1.pieces_ref), custom_call_target="tpu_custom_call" | custom-call | flops 62914560 | bytes 3932160 | tf_op jit(solution)/shard_map/pallas_call | solution.py:176
  56.2 0.0 collective-permute-done.16
  56.2 0.0 collective-permute-done.15
  56.2 0.6 collective-permute-done.14
  56.8 6.8 %shard_map.51 = f32[16,768]{1,0:T(8,128)S(1)} custom-call(s32[12]{0:T(128)S(1)} %pad_add_fusion.1.starts_ref, bf16[768,10240]{1,0:T(8,128)(2,1)} %tensor_ref.7, bf16[12,16,640]{2,1,0:T(8,128)(2,1)S(1)} %pad_maximum_fusion.pieces_ref, f32[16,768]{1,0:T(8,128)S(1)} %shard_map.50.rest_0_), custom_call_target="tpu_custom_call" | custom-call | flops 188743680 | bytes 11796480 | tf_op jit(solution)/shard_map/pallas_call | solution.py:176
  63.6 1.7 %collective-permute-start.17 = (f32[8,768]{1,0:T(8,128)S(1)}, f32[8,768]{1,0:T(8,128)S(1)}, u32[]{:S(2)}, u32[]{:S(2)}) collective-permute-start(f32[8,768]{1,0:T(8,128)S(1)} %constant_dynamic-slice_fusion), channel_id=1, source_target_pairs={{0,1},{1,0},{2,3},{3,2},{4,5},{5,4},{6,7},{7,6},{8,9},{9,8},{10,11... | collective-permute-start | bytes 73736 | tf_op jit(solution)/shard_map/ppermute | solution.py:28
  65.4 0.8 %collective-permute-done.17 = f32[8,768]{1,0:T(8,128)S(1)} collective-permute-done((f32[8,768]{1,0:T(8,128)S(1)}, f32[8,768]{1,0:T(8,128)S(1)}, u32[]{:S(2)}, u32[]{:S(2)}) %collective-permute-start.17) | collective-permute-done | bytes 24608 | tf_op jit(solution)/shard_map/ppermute | solution.py:28
  66.2 0.6 select_convert_fusion
  (8 shorter events, 0.1 us)
Async XLA Ops:
  0.7 0.7 %copy-start = (bf16[16,768]{1,0:T(8,128)(2,1)S(1)}, bf16[16,768]{1,0:T(8,128)(2,1)}, u32[]{:S(2)}) copy-start(bf16[16,768]{1,0:T(8,128)(2,1)} %dens_ref.3) | copy-start | bytes 73732
  6.2 6.9 %collective-permute-start.2 = (bf16[16,2560]{1,0:T(8,128)(2,1)S(1)}, bf16[16,2560]{1,0:T(8,128)(2,1)S(1)}, u32[]{:S(2)}, u32[]{:S(2)}) collective-permute-start(bf16[16,2560]{1,0:T(8,128)(2,1)S(1)} %get-tuple-element.10), channel_id=1, source_target_pairs={{0,2},{2,0},{4,6},{6,4},{8,10},{10,8},{12,14},{14,12},{16,18},{18,... | collective-permute-start | bytes 245768 | tf_op jit(solution)/shard_map/ppermute | solution.py:28
  9.2 5.3 %collective-permute-start.1 = (bf16[16,2560]{1,0:T(8,128)(2,1)S(1)}, bf16[16,2560]{1,0:T(8,128)(2,1)S(1)}, u32[]{:S(2)}, u32[]{:S(2)}) collective-permute-start(bf16[16,2560]{1,0:T(8,128)(2,1)S(1)} %get-tuple-element.9), channel_id=1, source_target_pairs={{0,4},{2,6},{4,0},{6,2},{8,12},{10,14},{12,8},{14,10},{16,20},{18,... | collective-permute-start | bytes 245768 | tf_op jit(solution)/shard_map/ppermute | solution.py:28
  10.7 5.3 %collective-permute-start = (bf16[16,2560]{1,0:T(8,128)(2,1)S(1)}, bf16[16,2560]{1,0:T(8,128)(2,1)S(1)}, u32[]{:S(2)}, u32[]{:S(2)}) collective-permute-start(bf16[16,2560]{1,0:T(8,128)(2,1)S(1)} %get-tuple-element.8), channel_id=1, source_target_pairs={{0,6},{2,4},{4,2},{6,0},{8,14},{10,12},{12,10},{14,8},{16,22},{18,... | collective-permute-start | bytes 245768 | tf_op jit(solution)/shard_map/ppermute | solution.py:28
  16.1 6.3 %collective-permute-start.5 = (bf16[16,2560]{1,0:T(8,128)(2,1)S(1)}, bf16[16,2560]{1,0:T(8,128)(2,1)S(1)}, u32[]{:S(2)}, u32[]{:S(2)}) collective-permute-start(bf16[16,2560]{1,0:T(8,128)(2,1)S(1)} %fusion), channel_id=1, source_target_pairs={{0,24},{2,26},{4,28},{6,30},{8,16},{10,18},{12,20},{14,22},{16,8},... | collective-permute-start | bytes 245768 | tf_op jit(solution)/shard_map/ppermute | solution.py:28
  19.8 5.7 %collective-permute-start.4 = (bf16[16,2560]{1,0:T(8,128)(2,1)S(1)}, bf16[16,2560]{1,0:T(8,128)(2,1)S(1)}, u32[]{:S(2)}, u32[]{:S(2)}) collective-permute-start(bf16[16,2560]{1,0:T(8,128)(2,1)S(1)} %fusion), channel_id=1, source_target_pairs={{0,16},{2,18},{4,20},{6,22},{8,24},{10,26},{12,28},{14,30},{16,0},... | collective-permute-start | bytes 245768 | tf_op jit(solution)/shard_map/ppermute | solution.py:28
  19.8 5.7 %collective-permute-start.3 = (bf16[16,2560]{1,0:T(8,128)(2,1)S(1)}, bf16[16,2560]{1,0:T(8,128)(2,1)S(1)}, u32[]{:S(2)}, u32[]{:S(2)}) collective-permute-start(bf16[16,2560]{1,0:T(8,128)(2,1)S(1)} %fusion), channel_id=1, source_target_pairs={{0,8},{2,10},{4,12},{6,14},{8,0},{10,2},{12,4},{14,6},{16,24},{18,... | collective-permute-start | bytes 245768 | tf_op jit(solution)/shard_map/ppermute | solution.py:28
  25.6 6.8 %collective-permute-start.6 = (bf16[16,2560]{1,0:T(8,128)(2,1)S(1)}, bf16[16,2560]{1,0:T(8,128)(2,1)S(1)}, u32[]{:S(2)}, u32[]{:S(2)}) collective-permute-start(bf16[16,2560]{1,0:T(8,128)(2,1)S(1)} %add_convert_fusion.rest_0_), channel_id=1, source_target_pairs={{0,6},{2,4},{4,2},{6,0},{8,14},{10,12},{12,10},{14,8},{16,22},{18,... | collective-permute-start | bytes 245768 | tf_op jit(solution)/shard_map/ppermute | solution.py:28
  26.7 5.7 %collective-permute-start.7 = (bf16[16,2560]{1,0:T(8,128)(2,1)S(1)}, bf16[16,2560]{1,0:T(8,128)(2,1)S(1)}, u32[]{:S(2)}, u32[]{:S(2)}) collective-permute-start(bf16[16,2560]{1,0:T(8,128)(2,1)S(1)} %add_convert_fusion.rest_0_), channel_id=1, source_target_pairs={{0,4},{2,6},{4,0},{6,2},{8,12},{10,14},{12,8},{14,10},{16,20},{18,... | collective-permute-start | bytes 245768 | tf_op jit(solution)/shard_map/ppermute | solution.py:28
  28.1 4.4 %collective-permute-start.8 = (bf16[16,2560]{1,0:T(8,128)(2,1)S(1)}, bf16[16,2560]{1,0:T(8,128)(2,1)S(1)}, u32[]{:S(2)}, u32[]{:S(2)}) collective-permute-start(bf16[16,2560]{1,0:T(8,128)(2,1)S(1)} %add_convert_fusion.rest_0_), channel_id=1, source_target_pairs={{0,2},{2,0},{4,6},{6,4},{8,10},{10,8},{12,14},{14,12},{16,18},{18,... | collective-permute-start | bytes 245768 | tf_op jit(solution)/shard_map/ppermute | solution.py:28
  39.6 1.3 %collective-permute-start.9 = (f32[16,640]{1,0:T(8,128)S(1)}, f32[16,640]{1,0:T(8,128)S(1)}, u32[]{:S(2)}, u32[]{:S(2)}) collective-permute-start(f32[16,640]{1,0:T(8,128)S(1)} %constant_dynamic-slice_fusion.1), channel_id=1, source_target_pairs={{0,1},{1,0},{2,3},{3,2},{4,5},{5,4},{6,7},{7,6},{8,9},{9,8},{10,11... | collective-permute-start | bytes 122888 | tf_op jit(solution)/shard_map/ppermute | solution.py:28
  40.9 6.9 %collective-permute-start.13 = (bf16[16,640]{1,0:T(8,128)(2,1)S(1)}, bf16[16,640]{1,0:T(8,128)(2,1)S(1)}, u32[]{:S(2)}, u32[]{:S(2)}) collective-permute-start(bf16[16,640]{1,0:T(8,128)(2,1)S(1)} %add_convert_fusion.1), channel_id=1, source_target_pairs={{0,24},{1,16},{8,8},{9,0},{16,25},{17,17},{24,9},{25,1},{2,26},{3,... | collective-permute-start | bytes 61448 | tf_op jit(solution)/shard_map/ppermute | solution.py:240
  45.1 3.8 %collective-permute-start.12 = (bf16[16,640]{1,0:T(8,128)(2,1)S(1)}, bf16[16,640]{1,0:T(8,128)(2,1)S(1)}, u32[]{:S(2)}, u32[]{:S(2)}) collective-permute-start(bf16[16,640]{1,0:T(8,128)(2,1)S(1)} %add_convert_fusion.1), channel_id=1, source_target_pairs={{0,16},{1,24},{8,0},{9,8},{16,17},{17,25},{24,1},{25,9},{2,18},{3,... | collective-permute-start | bytes 61448 | tf_op jit(solution)/shard_map/ppermute | solution.py:240
  45.5 3.5 %collective-permute-start.11 = (bf16[16,640]{1,0:T(8,128)(2,1)S(1)}, bf16[16,640]{1,0:T(8,128)(2,1)S(1)}, u32[]{:S(2)}, u32[]{:S(2)}) collective-permute-start(bf16[16,640]{1,0:T(8,128)(2,1)S(1)} %add_convert_fusion.1), channel_id=1, source_target_pairs={{0,8},{1,0},{8,24},{9,16},{16,9},{17,1},{24,25},{25,17},{2,10},{3,... | collective-permute-start | bytes 61448 | tf_op jit(solution)/shard_map/ppermute | solution.py:240
  47.2 1.8 %collective-permute-start.10 = (bf16[16,640]{1,0:T(8,128)(2,1)S(1)}, bf16[16,640]{1,0:T(8,128)(2,1)S(1)}, u32[]{:S(2)}, u32[]{:S(2)}) collective-permute-start(bf16[16,640]{1,0:T(8,128)(2,1)S(1)} %add_convert_fusion.1), channel_id=1, source_target_pairs={{0,0},{1,8},{8,16},{9,24},{16,1},{17,9},{24,17},{25,25},{2,2},{3,1... | collective-permute-start | bytes 61448 | tf_op jit(solution)/shard_map/ppermute | solution.py:240
  49.0 7.2 %collective-permute-start.16 = (bf16[4,16,640]{2,1,0:T(8,128)(2,1)S(1)}, bf16[4,16,640]{2,1,0:T(8,128)(2,1)S(1)}, u32[]{:S(2)}, u32[]{:S(2)}) collective-permute-start(bf16[4,16,640]{2,1,0:T(8,128)(2,1)S(1)} %pad_maximum_fusion.1.pieces_ref), channel_id=1, source_target_pairs={{0,2},{2,0},{4,6},{6,4},{8,10},{10,8},{12,14},{14,12},{16,18},{18,... | collective-permute-start | bytes 245768 | tf_op jit(solution)/shard_map/ppermute | solution.py:28
  50.1 6.1 %collective-permute-start.15 = (bf16[4,16,640]{2,1,0:T(8,128)(2,1)S(1)}, bf16[4,16,640]{2,1,0:T(8,128)(2,1)S(1)}, u32[]{:S(2)}, u32[]{:S(2)}) collective-permute-start(bf16[4,16,640]{2,1,0:T(8,128)(2,1)S(1)} %pad_maximum_fusion.1.pieces_ref), channel_id=1, source_target_pairs={{0,4},{2,6},{4,0},{6,2},{8,12},{10,14},{12,8},{14,10},{16,20},{18,... | collective-permute-start | bytes 245768 | tf_op jit(solution)/shard_map/ppermute | solution.py:28
  50.7 6.0 %collective-permute-start.14 = (bf16[4,16,640]{2,1,0:T(8,128)(2,1)S(1)}, bf16[4,16,640]{2,1,0:T(8,128)(2,1)S(1)}, u32[]{:S(2)}, u32[]{:S(2)}) collective-permute-start(bf16[4,16,640]{2,1,0:T(8,128)(2,1)S(1)} %pad_maximum_fusion.1.pieces_ref), channel_id=1, source_target_pairs={{0,6},{2,4},{4,2},{6,0},{8,14},{10,12},{12,10},{14,8},{16,22},{18,... | collective-permute-start | bytes 245768 | tf_op jit(solution)/shard_map/ppermute | solution.py:28
  63.6 2.6 %collective-permute-start.17 = (f32[8,768]{1,0:T(8,128)S(1)}, f32[8,768]{1,0:T(8,128)S(1)}, u32[]{:S(2)}, u32[]{:S(2)}) collective-permute-start(f32[8,768]{1,0:T(8,128)S(1)} %constant_dynamic-slice_fusion), channel_id=1, source_target_pairs={{0,1},{1,0},{2,3},{3,2},{4,5},{5,4},{6,7},{7,6},{8,9},{9,8},{10,11... | collective-permute-start | bytes 73736 | tf_op jit(solution)/shard_map/ppermute | solution.py:28

commit v2 on v0

v2 whole, which is shorter than its diff:
```python
import functools

import jax
import jax.numpy as jnp
from jax import lax
from jax.experimental import pallas as pl
from jax.experimental.pallas import tpu as pltpu
from jax.sharding import PartitionSpec as P

F32, BF16 = jnp.float32, jnp.bfloat16
MIB = 1 << 20


def digits_of(count):
    sizes = []
    while count > 1:
        size = 4 if count % 4 == 0 else 2
        sizes.append(size)
        count //= size
    return sizes


def largest_step(extent, limit, unit):
    return max(s for s in range(unit, limit + 1, unit) if extent % s == 0)


def swap(x, axis, count, mask):
    return lax.ppermute(x, axis, [(i, i ^ mask) for i in range(count)])


def params(used_bytes):
    return pltpu.CompilerParams(vmem_limit_bytes=used_bytes + 4 * MIB)


def in_hbm(x):
    return pltpu.with_memory_space_constraint(x, pltpu.HBM)


def in_vmem(x):
    return pltpu.with_memory_space_constraint(x, pltpu.VMEM)


def spec(space):
    return pl.BlockSpec(memory_space=space)


SMEM, VMEM, HBM = pltpu.SMEM, pltpu.VMEM, pltpu.HBM


def cost(flops, read):
    return pl.CostEstimate(flops=flops, bytes_accessed=read, transcendentals=0)


def slot_copies(digit, picks, per, tensor_ref, slots_ref, sems):
    step = slots_ref.shape[2]
    copies = []
    for at, pick in enumerate(picks):
        for j in range(per):
            slot = (digit ^ pick) * per + j
            copy = pltpu.make_async_copy(
                tensor_ref.at[:, pl.ds(pl.multiple_of(slot * step, 128), step)],
                slots_ref.at[slot],
                sems.at[at * per + j],
            )
            copy.start()
            copies.append((copy, slot))
    return copies


def fit_terms(masked, copies, per, slots_ref, outs):
    step = slots_ref.shape[2]
    for i, (copy, slot) in enumerate(copies):
        copy.wait()
        term = jnp.dot(masked, slots_ref[slot], preferred_element_type=F32)
        out, j = outs[i // per], i % per
        out[:, j * step : (j + 1) * step] = term.astype(out.dtype)


def fit_others_kernel(picks, per, info_ref, dens_hbm, tensor_ref, *rest):
    outs, (masked_ref, slots_ref, dens_ref, dens_sem, sems) = rest[: len(picks)], rest[len(picks) :]
    first = pltpu.make_async_copy(dens_hbm, dens_ref, dens_sem)
    first.start()
    copies = slot_copies(info_ref[0] & len(picks), picks, per, tensor_ref, slots_ref, sems)
    first.wait()
    dens = dens_ref[...]
    live = lax.broadcasted_iota(jnp.int32, dens.shape, 1) < info_ref[2]
    masked = jnp.where(live, dens.astype(F32), 0.0).astype(BF16)
    masked_ref[...] = masked
    fit_terms(masked, copies, per, slots_ref, outs)


def fit_others(picks, per, step, info, densities, tensor):
    rows, half_aux = tensor.shape
    k = densities.shape[0]
    n = len(picks) * per
    return pl.pallas_call(
        functools.partial(fit_others_kernel, picks, per),
        out_shape=[jax.ShapeDtypeStruct((k, per * step), BF16) for _ in picks]
        + [jax.ShapeDtypeStruct((k, rows), BF16), VMEM((half_aux // step, rows, step), BF16)],
        in_specs=[spec(SMEM), spec(HBM), spec(HBM)],
        out_specs=[spec(VMEM) for _ in range(len(picks) + 2)],
        scratch_shapes=[
            VMEM((k, rows), BF16),
            pltpu.SemaphoreType.DMA,
            pltpu.SemaphoreType.DMA((n,)),
        ],
        compiler_params=params(0),
        cost_estimate=cost(2 * k * rows * step * n, n * rows * step * 2),
    )(info, in_hbm(densities), in_hbm(tensor))


def row_copies(digit, picks, metric_ref, held, sems):
    depth = held[0].shape[0]
    copies = []
    for at, pick in enumerate(picks):
        first = pl.multiple_of((digit ^ pick) * depth, 128)
        copy = pltpu.make_async_copy(metric_ref.at[pl.ds(first, depth), :], held[at], sems.at[at])
        copy.start()
        copies.append(copy)
    return copies


def fit_own_kernel(
    per, top, info_ref, masked_ref, tensor_ref, metric_ref, before_ref, *rest
):
    out_ref, slots_ref, held_ref, sems, row_sems = rest
    digit = info_ref[0] & top
    copies = slot_copies(digit, [0], per, tensor_ref, slots_ref, sems)
    (rows_in,) = row_copies(digit, [0], metric_ref, [held_ref], row_sems)
    fit_terms(masked_ref[...], copies, per, slots_ref, [out_ref])
    rows_in.wait()


def fit_own(per, top, step, info, masked, tensor, metric, slots):
    rows = tensor.shape[0]
    k = masked.shape[0]
    depth, width = per * step, metric.shape[1]
    return pl.pallas_call(
        functools.partial(fit_own_kernel, per, top),
        out_shape=[
            jax.ShapeDtypeStruct((k, per * step), F32),
            VMEM(slots.shape, BF16),
            VMEM((depth, width), BF16),
        ],
        in_specs=[spec(SMEM), spec(VMEM), spec(HBM), spec(HBM), spec(VMEM)],
        out_specs=[spec(VMEM) for _ in range(3)],
        scratch_shapes=[pltpu.SemaphoreType.DMA((per,)), pltpu.SemaphoreType.DMA((1,))],
        input_output_aliases={4: 1},
        compiler_params=params(0),
        cost_estimate=cost(2 * k * rows * step * per, (per * rows * step + depth * width) * 2),
    )(info, masked, in_hbm(tensor), in_hbm(metric), in_vmem(slots))


def fetch_kernel(picks, top, info_ref, metric_ref, own_ref, *rest):
    *held, same_ref, sems = rest
    copies = row_copies(info_ref[0] & top, picks, metric_ref, held, sems)
    same_ref[...] = own_ref[...]
    for copy in copies:
        copy.wait()


def fetch(picks, top, depth, info, metric, own):
    width = metric.shape[1]
    return pl.pallas_call(
        functools.partial(fetch_kernel, picks, top),
        out_shape=[VMEM((depth, width), BF16) for _ in picks]
        + [jax.ShapeDtypeStruct(own.shape, own.dtype)],
        in_specs=[spec(SMEM), spec(HBM), spec(VMEM)],
        out_specs=[spec(VMEM) for _ in range(len(picks) + 1)],
        scratch_shapes=[pltpu.SemaphoreType.DMA((len(picks),))],
        compiler_params=params(0),
        cost_estimate=cost(0, len(picks) * depth * width * 2),
    )(info, in_hbm(metric), own)


def solve_own_kernel(
    picks, top, info_ref, metric_ref, fitted_ref, held_ref, out_ref, *rest
):
    *late, sems = rest
    copies = row_copies(info_ref[0] & top, picks, metric_ref, late, sems)
    out_ref[...] = jnp.dot(fitted_ref[...], held_ref[...], preferred_element_type=F32)
    for copy in copies:
        copy.wait()


def solve_own(picks, top, info, metric, fitted, held):
    k, depth = fitted.shape
    width = metric.shape[1]
    return pl.pallas_call(
        functools.partial(solve_own_kernel, picks, top),
        out_shape=[jax.ShapeDtypeStruct((k, width), F32)]
        + [VMEM((depth, width), BF16) for _ in picks],
        in_specs=[spec(SMEM), spec(HBM), spec(VMEM), spec(VMEM)],
        out_specs=[spec(VMEM) for _ in range(len(picks) + 1)],
        scratch_shapes=[pltpu.SemaphoreType.DMA((len(picks),))],
        compiler_params=params(0),
        cost_estimate=cost(2 * k * depth * width, (1 + len(picks)) * depth * width * 2),
    )(info, in_hbm(metric), fitted, in_vmem(held))


def solve_others_kernel(count, low, info_ref, begun_ref, *rest):
    fitted, held, (out_ref, home_ref) = rest[:count], rest[count : 2 * count], rest[2 * count :]
    total = begun_ref[...]
    for x, rows in zip(fitted, held):
        total += jnp.dot(x[...], rows[...], preferred_element_type=F32)
    out_ref[...] = total
    home = info_ref[0] >> (low.bit_length()) == info_ref[1]
    home_ref[...] = jnp.where(home, total, 0.0)


def solve_others(low, info, begun, fitted, held):
    k, depth = fitted[0].shape
    width = held[0].shape[1]
    count = len(fitted)
    return pl.pallas_call(
        functools.partial(solve_others_kernel, count, low),
        out_shape=[VMEM((k, width), F32) for _ in range(2)],
        in_specs=[spec(SMEM)] + [spec(VMEM) for _ in range(1 + 2 * count)],
        out_specs=[spec(VMEM), spec(VMEM)],
        compiler_params=params(0),
        cost_estimate=cost(2 * k * depth * width * count, count * depth * width * 2),
    )(info, begun, *fitted, *[in_vmem(x) for x in held])


def split_for_cores(total, axis, core, outs):
    if len(outs) == 1:
        outs[0][...] = total
        return
    low, high = jnp.split(total, 2, axis)
    outs[0][...] = jnp.where(core == 0, low, high)
    outs[1][...] = jnp.where(core == 0, high, low)


def back_kernel(which, begun, low, info_ref, slots_ref, *rest):
    pieces, rest = rest[: len(which)], rest[len(which) :]
    if begun:
        start_ref, *outs = rest
        total = start_ref[...]
    else:
        outs = rest
        total = jnp.zeros((pieces[0].shape[1], slots_ref.shape[1]), F32)
    line, mine = info_ref[0] & (low - 1), info_ref[0] >> (low.bit_length() - 1)
    step = slots_ref.shape[2]
    for part, place in zip(pieces, which):
        per = part.shape[2] // step
        for i in range(part.shape[0]):
            for j in range(per):
                slot = i
                if place is not None:
                    slot = (((mine ^ i) & 1) * low + (line ^ place)) * per + j
                total += lax.dot_general(
                    part[i, :, j * step : (j + 1) * step],
                    slots_ref[slot],
                    (((1,), (1,)), ((), ())),
                    preferred_element_type=F32,
                )
    split_for_cores(total, 0, info_ref[1], outs)


def back(which, low, info, slots, pieces, begun=None, split=True):
    rows = slots.shape[1]
    _, k, width = pieces[0].shape
    count = sum(part.shape[0] for part in pieces)
    extra = [] if begun is None else [begun]
    shapes = [(k // 2, rows)] * 2 if split else [(k, rows)]
    return pl.pallas_call(
        functools.partial(back_kernel, which, begun is not None, low),
        out_shape=[jax.ShapeDtypeStruct(shape, F32) for shape in shapes],
        in_specs=[spec(SMEM), spec(VMEM)] + [spec(VMEM) for _ in pieces + extra],
        out_specs=[spec(VMEM) for _ in shapes],
        compiler_params=params(0),
        cost_estimate=cost(2 * k * rows * width * count, count * rows * width * 2),
    )(info, in_vmem(slots), *pieces, *extra)


def body(n_pairs, densities, tensor, metric, row_count):
    rows, half_aux = tensor.shape
    block = metric.shape[1]
    sizes = digits_of(n_pairs)
    me = lax.axis_index("pairs")
    core = lax.axis_index("aux")
    first, rest = sizes[0], sizes[1:]
    info = jnp.stack([me.astype(jnp.int32), core.astype(jnp.int32), row_count[0]])
    width = half_aux // first

    others = list(range(first - 1, 0, -1))
    step = largest_step(width, 640, 128)
    per = width // step
    *sent, masked, slots = fit_others(others, per, step, info, densities, tensor)
    arrived = [swap(x, "pairs", n_pairs, pick) for x, pick in zip(sent, others)]
    total, slots, held = fit_own(per, first - 1, step, info, masked, tensor, metric, slots)
    for x in arrived:
        total = total + x.astype(F32)
    here = len(others) - 1
    stride = first
    for size in rest:
        sending = total.astype(BF16)
        arrived = [swap(sending, "pairs", n_pairs, pick * stride) for pick in range(1, size)]
        if stride == first:
            *rows_of, total = fetch(others[:here], first - 1, width, info, metric, total)
        for x in arrived:
            total = total + x.astype(F32)
        stride *= size
    fitted = total.astype(BF16)

    gathered = [swap(fitted, "pairs", n_pairs, pick) for pick in others]
    part, *late = solve_own(others[here:], first - 1, info, metric, fitted, held)
    last = sizes[-1]
    low = n_pairs // last
    part, at_home = solve_others(low, info, part, gathered, rows_of + late)

    homes = [(p, (p // low) // 2) for p in range(n_pairs)]
    across = 2 * low

    def send(x, pairs):
        return lax.ppermute(x, ("pairs", "aux"), [(p * 2 + c, q * 2 + d) for p, c, q, d in pairs])

    term = part.astype(BF16)
    first_pairs = [(p, 1 - c, p, c) for p, c in homes] + [(p, c, p ^ across, c) for p, c in homes]
    other_term = send(term, first_pairs)
    third_term = send(term, [(p, 1 - c, p ^ across, c) for p, c in homes])
    own = (at_home + other_term.astype(F32) + third_term.astype(F32)).astype(BF16)
    line_blocks = jnp.stack([own, swap(own, "pairs", n_pairs, low)])

    if block % step == 0 and len(sizes) == 2:
        arrived = [swap(line_blocks, "pairs", n_pairs, pick) for pick in others]
        (begun,) = back([0], low, info, slots, [line_blocks], split=False)
        (begun,) = back(others[:1], low, info, slots, arrived[:1], begun, split=False)
        keep, give = back(others[1:], low, info, slots, arrived[1:], begun)
    else:
        mine = me // low
        origin = [((mine ^ i) & 1) * low * block for i in range(2)]
        stride = 1
        lines = [me % low]
        pieces = line_blocks[None]
        for size in sizes[:-1]:
            arrived = [pieces] + [swap(pieces, "pairs", n_pairs, pick * stride) for pick in range(1, size)]
            lines = [x ^ (pick * stride) for pick in range(size) for x in lines]
            pieces = jnp.concatenate(arrived)
            stride *= size
        whole = jnp.zeros((densities.shape[0], half_aux), BF16)
        for at, x in enumerate(lines):
            for i in range(2):
                whole = lax.dynamic_update_slice_in_dim(
                    whole, pieces[at, i], origin[i] + x * block, 1
                )
        count = half_aux // step
        pieces = whole.reshape(-1, count, step).transpose(1, 0, 2)
        keep, give = back([None], low, info, slots, [pieces])

    coulomb = keep + swap(give, "aux", 2, 1)
    live = lax.broadcasted_iota(jnp.int32, (1, rows), 1) < row_count[0]
    return jnp.where(live, coulomb, 0.0).astype(BF16)


def solution(mesh):
    placed = (P(None, "pairs"), P("pairs", "aux"), P("aux", "pairs"), P("pairs"))
    return jax.shard_map(
        functools.partial(body, mesh.shape["pairs"]),
        mesh=mesh,
        in_specs=placed,
        out_specs=P("aux", "pairs"),
        check_vma=False,
    )
```

time: 178 us -> 59 us (0.33)
  blocking collectives: 129 us -> 0 us
  matrix products: 28.2 us -> 0 us
  Pallas kernels: 0 us -> 27.9 us
  starting transfers between devices: 0.01 us -> 22.4 us
  between operations: 14.1 us -> 0.77 us
    psum x2 -> x0, blocking collectives: 89.9 us -> none  [the longest x1 86.2 us: body(): fitted = lax.psum(fit_part, 'pairs').astype(jnp.bfloat16)]
    all_gather x1 -> x0, blocking collectives: 39.1 us -> none  [body(): solved = lax.all_gather(summed, 'pairs', axis=1, tiled=True)]
    dot_general x3 -> x0, matrix products: 28.2 us -> none  [the longest x1 10.3 us: body(): lax.dot_general(own_block, tensor, (((1,), (1,)), ((), ())), preferred_el...]
    pallas_call x0 -> x8, Pallas kernels: none -> 27.9 us  [the longest x3 6 us: back(): pl.pallas_call(functools.partial(back_kernel, which, begun is not None, l...]
    ppermute x0 -> x16, starting transfers between devices: none -> 22.4 us  [the longest x14 18.4 us: swap(): return lax.ppermute(x, axis, [(i, i ^ mask) for i in range(count)])]
    ppermute x0 -> x16, waiting for transfers between devices: none -> 6.95 us  [the longest x14 5.28 us: swap(): return lax.ppermute(x, axis, [(i, i ^ mask) for i in range(count)])]
    reduce_scatter x1 -> x0, waiting for transfers between devices: 5.44 us -> none  [body(): lax.psum_scatter(back_term, 'aux', scatter_dimension=0, tiled=True)]
  transfers between devices with their start and end apart: 1 -> 16, of which waited for: 1 -> 8; matrix products, arithmetic and copies ran while one was open for 0% -> 0% of each run, Pallas kernels for 0% -> 28%
where the time goes in v2:
time: 59 us; the launch traced here: 58.9 us
  Pallas kernels  27.9 us (47%)
  starting transfers between devices  22.4 us (38%)
  waiting for transfers between devices  6.95 us (12%)
  other arithmetic  0.82 us (1%)
  between operations  0.77 us (1%)
    ppermute x14, starting transfers between devices, swap(): return lax.ppermute(x, axis, [(i, i ^ mask) for i in range(count)])  18.4 us
    pallas_call x3, Pallas kernels, back(): pl.pallas_call(functools.partial(back_kernel, which, begun is not None, l...  6 us
    pallas_call x1, Pallas kernels, fit_others(): pl.pallas_call(functools.partial(fit_others_kernel, picks, per), out_shap...  5.36 us
    pallas_call x1, Pallas kernels, fetch(): pl.pallas_call(functools.partial(fetch_kernel, picks, top), out_shape=[VM...  5.3 us
    ppermute x14, waiting for transfers between devices, swap(): return lax.ppermute(x, axis, [(i, i ^ mask) for i in range(count)])  5.28 us
    pallas_call x1, Pallas kernels, fit_own(): pl.pallas_call(functools.partial(fit_own_kernel, per, top), out_shape=[ja...  4.68 us
    ppermute x2, starting transfers between devices, send(): lax.ppermute(x, ('pairs', 'aux'), [(p * 2 + c, q * 2 + d) for p, c, q, d...  4.02 us
    pallas_call x1, Pallas kernels, solve_own(): pl.pallas_call(functools.partial(solve_own_kernel, picks, top), out_shape...  3.43 us
  transfers between devices with their start and end apart: 16, of which 8 were waited for; matrix products, arithmetic and copies ran while one was open for 0% of the time, Pallas kernels for 28%

profile of v2, /device:TPU:0, one launch (start us, length us, event | category | flops | bytes accessed | tf_op | source)
XLA Modules:
  0.0 58.9 jit_solution(12452175998344482508)
XLA Ops:
  0.7 0.1 pad_add_fusion.info_ref
  0.7 5.4 %shard_map.46 = (bf16[16,2560]{1,0:T(8,128)(2,1)S(1)}, bf16[16,2560]{1,0:T(8,128)(2,1)S(1)}, bf16[16,2560]{1,0:T(8,128)(2,1)S(1)}, bf16[16,768]{1,0:T(8,128)(2,1)S(1)}, bf16[16,768,640]{2,1,0:T(8,128)(2,1)S(1)}) custom-call(s32[3]{0:T(128)S(1)} %pad_add_fusion.info_ref, bf16[16,768]{1,0:T(8,128)(2,1)} %dens_hbm.1, bf16[768,10240]{1,0:T(8,128)(2,1)} %tensor_ref.3), custom_call_target="tpu_custom_call" | custom-call | flops 188743680 | bytes 11796480 | tf_op jit(solution)/shard_map/pallas_call | solution.py:96
  6.1 3.0 %collective-permute-start.2 = (bf16[16,2560]{1,0:T(8,128)(2,1)S(1)}, bf16[16,2560]{1,0:T(8,128)(2,1)S(1)}, u32[]{:S(2)}, u32[]{:S(2)}) collective-permute-start(bf16[16,2560]{1,0:T(8,128)(2,1)S(1)} %get-tuple-element.28), channel_id=1, source_target_pairs={{0,2},{2,0},{4,6},{6,4},{8,10},{10,8},{12,14},{14,12},{16,18},{18,... | collective-permute-start | bytes 245768 | tf_op jit(solution)/shard_map/ppermute | solution.py:28
  9.1 1.5 %collective-permute-start.1 = (bf16[16,2560]{1,0:T(8,128)(2,1)S(1)}, bf16[16,2560]{1,0:T(8,128)(2,1)S(1)}, u32[]{:S(2)}, u32[]{:S(2)}) collective-permute-start(bf16[16,2560]{1,0:T(8,128)(2,1)S(1)} %get-tuple-element.27), channel_id=1, source_target_pairs={{0,4},{2,6},{4,0},{6,2},{8,12},{10,14},{12,8},{14,10},{16,20},{18,... | collective-permute-start | bytes 245768 | tf_op jit(solution)/shard_map/ppermute | solution.py:28
  10.6 0.0 collective-permute-start
  10.6 4.7 %shard_map.47 = (f32[16,2560]{1,0:T(8,128)S(1)}, bf16[16,768,640]{2,1,0:T(8,128)(2,1)S(1)}, bf16[2560,1280]{1,0:T(8,128)(2,1)S(1)}) custom-call(s32[3]{0:T(128)S(1)} %pad_add_fusion.info_ref, bf16[16,768]{1,0:T(8,128)(2,1)S(1)} %get-tuple-element.22.masked_ref, bf16[768,10240]{1,0:T(8,128)(2,1)} %tensor_ref.3, ...), custom_call_target="tpu_custom_call", output_to_operand_aliasing={{1}: (4, {})} | custom-call | flops 62914560 | bytes 10485760 | tf_op jit(solution)/shard_map/pallas_call | solution.py:138
  15.3 0.0 collective-permute-done.2
  15.3 0.0 collective-permute-done.1
  15.4 0.6 %collective-permute-done = bf16[16,2560]{1,0:T(8,128)(2,1)S(1)} collective-permute-done((bf16[16,2560]{1,0:T(8,128)(2,1)S(1)}, bf16[16,2560]{1,0:T(8,128)(2,1)S(1)}, u32[]{:S(2)}, u32[]{:S(2)}) %collective-permute-start) | collective-permute-done | bytes 81952 | tf_op jit(solution)/shard_map/ppermute | solution.py:28
  16.0 3.7 %collective-permute-start.5 = (bf16[16,2560]{1,0:T(8,128)(2,1)S(1)}, bf16[16,2560]{1,0:T(8,128)(2,1)S(1)}, u32[]{:S(2)}, u32[]{:S(2)}) collective-permute-start(bf16[16,2560]{1,0:T(8,128)(2,1)S(1)} %get-tuple-element.39), channel_id=1, source_target_pairs={{0,24},{2,26},{4,28},{6,30},{8,16},{10,18},{12,20},{14,22},{16,8},... | collective-permute-start | bytes 245768 | tf_op jit(solution)/shard_map/ppermute | solution.py:28
  19.7 0.0 collective-permute-start.4
  19.7 0.8 %collective-permute-start.3 = (bf16[16,2560]{1,0:T(8,128)(2,1)S(1)}, bf16[16,2560]{1,0:T(8,128)(2,1)S(1)}, u32[]{:S(2)}, u32[]{:S(2)}) collective-permute-start(bf16[16,2560]{1,0:T(8,128)(2,1)S(1)} %get-tuple-element.39), channel_id=1, source_target_pairs={{0,8},{2,10},{4,12},{6,14},{8,0},{10,2},{12,4},{14,6},{16,24},{18,... | collective-permute-start | bytes 245768 | tf_op jit(solution)/shard_map/ppermute | solution.py:28
  20.5 5.3 %shard_map.48 = (bf16[2560,1280]{1,0:T(8,128)(2,1)S(1)}, bf16[2560,1280]{1,0:T(8,128)(2,1)S(1)}, f32[16,2560]{1,0:T(8,128)S(1)}) custom-call(s32[3]{0:T(128)S(1)} %pad_add_fusion.info_ref, bf16[10240,1280]{1,0:T(8,128)(2,1)} %metric_ref.5, f32[16,2560]{1,0:T(8,128)S(1)} %get-tuple-element.40.own_ref), custom_call_target="tpu_custom_call" | custom-call | bytes 13107200 | tf_op jit(solution)/shard_map/pallas_call | solution.py:164
  25.8 0.0 collective-permute-done.5
  25.8 0.1 collective-permute-done.4
  25.9 0.0 collective-permute-done.3
  26.0 2.4 %collective-permute-start.6 = (bf16[16,2560]{1,0:T(8,128)(2,1)S(1)}, bf16[16,2560]{1,0:T(8,128)(2,1)S(1)}, u32[]{:S(2)}, u32[]{:S(2)}) collective-permute-start(bf16[16,2560]{1,0:T(8,128)(2,1)S(1)} %add_convert_fusion.fitted_ref), channel_id=1, source_target_pairs={{0,6},{2,4},{4,2},{6,0},{8,14},{10,12},{12,10},{14,8},{16,22},{18,... | collective-permute-start | bytes 245768 | tf_op jit(solution)/shard_map/ppermute | solution.py:28
  28.3 0.5 collective-permute-start.7
  28.8 0.7 %collective-permute-start.8 = (bf16[16,2560]{1,0:T(8,128)(2,1)S(1)}, bf16[16,2560]{1,0:T(8,128)(2,1)S(1)}, u32[]{:S(2)}, u32[]{:S(2)}) collective-permute-start(bf16[16,2560]{1,0:T(8,128)(2,1)S(1)} %add_convert_fusion.fitted_ref), channel_id=1, source_target_pairs={{0,2},{2,0},{4,6},{6,4},{8,10},{10,8},{12,14},{14,12},{16,18},{18,... | collective-permute-start | bytes 245768 | tf_op jit(solution)/shard_map/ppermute | solution.py:28
  29.5 3.4 %shard_map.49 = (f32[16,1280]{1,0:T(8,128)S(1)}, bf16[2560,1280]{1,0:T(8,128)(2,1)S(1)}) custom-call(s32[3]{0:T(128)S(1)} %pad_add_fusion.info_ref, bf16[10240,1280]{1,0:T(8,128)(2,1)} %metric_ref.5, bf16[16,2560]{1,0:T(8,128)(2,1)S(1)} %add_convert_fusion.fitted_ref, bf16[2560,1280]{1,0:T(8,128)(2,1)S(1)} %get-tuple-element.30.held_ref), custom_call_target="tpu_custom_call" | custom-call | flops 104857600 | bytes 13107200 | tf_op jit(solution)/shard_map/pallas_call | solution.py:189
  33.0 0.0 collective-permute-done.6.rest_0_
  33.0 0.0 collective-permute-done.7.rest_1_
  33.0 0.3 collective-permute-done.8.rest_2_
  33.3 3.2 %shard_map.50 = (f32[16,1280]{1,0:T(8,128)S(1)}, f32[16,1280]{1,0:T(8,128)S(1)}) custom-call(s32[3]{0:T(128)S(1)} %pad_add_fusion.info_ref, f32[16,1280]{1,0:T(8,128)S(1)} %get-tuple-element.31.begun_ref, bf16[16,2560]{1,0:T(8,128)(2,1)S(1)} %collective-permute-done.6.rest_0_, bf16[16,2560]{1,0:T(8,128)(2,1)S(1)} %collective-permute-done.7.rest_1_, ...), custom_call_target="tpu_custom_call" | custom-call | flops 314572800 | bytes 19660800 | tf_op jit(solution)/shard_map/pallas_call | solution.py:215
  36.5 0.7 %collective-permute-start.10 = (bf16[16,1280]{1,0:T(8,128)(2,1)S(1)}, bf16[16,1280]{1,0:T(8,128)(2,1)S(1)}, u32[]{:S(2)}, u32[]{:S(2)}) collective-permute-start(bf16[16,1280]{1,0:T(8,128)(2,1)S(1)} %convert_element_type.47), channel_id=1, source_target_pairs={{1,16},{3,18},{5,20},{7,22},{9,24},{11,26},{13,28},{15,30},{16,1},... | collective-permute-start | bytes 122888 | tf_op jit(solution)/shard_map/ppermute | solution.py:316
  37.2 3.4 %collective-permute-start.9 = (bf16[16,1280]{1,0:T(8,128)(2,1)S(1)}, bf16[16,1280]{1,0:T(8,128)(2,1)S(1)}, u32[]{:S(2)}, u32[]{:S(2)}) collective-permute-start(bf16[16,1280]{1,0:T(8,128)(2,1)S(1)} %convert_element_type.47), channel_id=1, source_target_pairs={{1,0},{3,2},{5,4},{7,6},{9,8},{11,10},{13,12},{15,14},{16,17},{18,... | collective-permute-start | bytes 122888 | tf_op jit(solution)/shard_map/ppermute | solution.py:316
  40.5 0.0 collective-permute-done.10
  40.5 1.7 %collective-permute-done.9 = bf16[16,1280]{1,0:T(8,128)(2,1)S(1)} collective-permute-done((bf16[16,1280]{1,0:T(8,128)(2,1)S(1)}, bf16[16,1280]{1,0:T(8,128)(2,1)S(1)}, u32[]{:S(2)}, u32[]{:S(2)}) %collective-permute-start.9) | collective-permute-done | bytes 40992 | tf_op jit(solution)/shard_map/ppermute | solution.py:316
  42.2 2.1 %collective-permute-start.11 = (bf16[16,1280]{1,0:T(8,128)(2,1)S(1)}, bf16[16,1280]{1,0:T(8,128)(2,1)S(1)}, u32[]{:S(2)}, u32[]{:S(2)}) collective-permute-start(bf16[16,1280]{1,0:T(8,128)(2,1)S(1)} %add_convert_fusion.1), channel_id=1, source_target_pairs={{0,8},{2,10},{4,12},{6,14},{8,0},{10,2},{12,4},{14,6},{16,24},{18,... | collective-permute-start | bytes 122888 | tf_op jit(solution)/shard_map/ppermute | solution.py:28
  44.4 2.0 %collective-permute-done.11 = bf16[16,1280]{1,0:T(8,128)(2,1)S(1)} collective-permute-done((bf16[16,1280]{1,0:T(8,128)(2,1)S(1)}, bf16[16,1280]{1,0:T(8,128)(2,1)S(1)}, u32[]{:S(2)}, u32[]{:S(2)}) %collective-permute-start.11) | collective-permute-done | bytes 40992 | tf_op jit(solution)/shard_map/ppermute | solution.py:28
  46.3 2.1 %collective-permute-start.14 = (bf16[2,16,1280]{2,1,0:T(8,128)(2,1)S(1)}, bf16[2,16,1280]{2,1,0:T(8,128)(2,1)S(1)}, u32[]{:S(2)}, u32[]{:S(2)}) collective-permute-start(bf16[2,16,1280]{2,1,0:T(8,128)(2,1)S(1)} %pad_maximum_fusion.rest_0_), channel_id=1, source_target_pairs={{0,6},{2,4},{4,2},{6,0},{8,14},{10,12},{12,10},{14,8},{16,22},{18,... | collective-permute-start | bytes 245768 | tf_op jit(solution)/shard_map/ppermute | solution.py:28
  48.4 0.5 collective-permute-start.12
  48.9 1.0 %collective-permute-start.13 = (bf16[2,16,1280]{2,1,0:T(8,128)(2,1)S(1)}, bf16[2,16,1280]{2,1,0:T(8,128)(2,1)S(1)}, u32[]{:S(2)}, u32[]{:S(2)}) collective-permute-start(bf16[2,16,1280]{2,1,0:T(8,128)(2,1)S(1)} %pad_maximum_fusion.rest_0_), channel_id=1, source_target_pairs={{0,2},{2,0},{4,6},{6,4},{8,10},{10,8},{12,14},{14,12},{16,18},{18,... | collective-permute-start | bytes 245768 | tf_op jit(solution)/shard_map/ppermute | solution.py:28
  49.9 1.7 %shard_map.51.rest_1_ = f32[16,768]{1,0:T(8,128)S(1)} custom-call(s32[3]{0:T(128)S(1)} %pad_add_fusion.info_ref, bf16[16,768,640]{2,1,0:T(8,128)(2,1)S(1)} %get-tuple-element.24.slots_ref, bf16[2,16,1280]{2,1,0:T(8,128)(2,1)S(1)} %pad_maximum_fusion.rest_0_), custom_call_target="tpu_custom_call" | custom-call | flops 62914560 | bytes 3932160 | tf_op jit(solution)/shard_map/pallas_call | solution.py:266
  51.6 0.8 %collective-permute-done.14.rest_0_ = bf16[2,16,1280]{2,1,0:T(8,128)(2,1)S(1)} collective-permute-done((bf16[2,16,1280]{2,1,0:T(8,128)(2,1)S(1)}, bf16[2,16,1280]{2,1,0:T(8,128)(2,1)S(1)}, u32[]{:S(2)}, u32[]{:S(2)}) %collective-permute-start.14) | collective-permute-done | bytes 81952 | tf_op jit(solution)/shard_map/ppermute | solution.py:28
  52.4 1.7 %shard_map.52.rest_2_ = f32[16,768]{1,0:T(8,128)S(1)} custom-call(s32[3]{0:T(128)S(1)} %pad_add_fusion.info_ref, bf16[16,768,640]{2,1,0:T(8,128)(2,1)S(1)} %get-tuple-element.24.slots_ref, bf16[2,16,1280]{2,1,0:T(8,128)(2,1)S(1)} %collective-permute-done.14.rest_0_, f32[16,768]{1,0:T(8,128)S(1)} %shard_map.51.rest_1_), custom_call_target="tpu_custom_call" | custom-call | flops 62914560 | bytes 3932160 | tf_op jit(solution)/shard_map/pallas_call | solution.py:266
  54.0 0.3 collective-permute-done.12.rest_0_
  54.4 0.0 collective-permute-done.13.rest_1_
  54.4 2.7 %shard_map.53 = (f32[8,768]{1,0:T(8,128)S(1)}, f32[8,768]{1,0:T(8,128)S(1)}) custom-call(s32[3]{0:T(128)S(1)} %pad_add_fusion.info_ref, bf16[16,768,640]{2,1,0:T(8,128)(2,1)S(1)} %get-tuple-element.24.slots_ref, bf16[2,16,1280]{2,1,0:T(8,128)(2,1)S(1)} %collective-permute-done.12.rest_0_, bf16[2,16,1280]{2,1,0:T(8,128)(2,1)S(1)} %collective-permute-done.13.rest_1_, ...), custom_call_target="tpu_custom_call" | custom-call | flops 125829120 | bytes 7864320 | tf_op jit(solution)/shard_map/pallas_call | solution.py:266
  57.1 0.1 collective-permute-start.15
  57.2 1.1 %collective-permute-done.15 = f32[8,768]{1,0:T(8,128)S(1)} collective-permute-done((f32[8,768]{1,0:T(8,128)S(1)}, f32[8,768]{1,0:T(8,128)S(1)}, u32[]{:S(2)}, u32[]{:S(2)}) %collective-permute-start.15) | collective-permute-done | bytes 24608 | tf_op jit(solution)/shard_map/ppermute | solution.py:28
  58.3 0.6 %select_convert_fusion = bf16[8,768]{1,0:T(8,128)(2,1)} fusion(f32[8,768]{1,0:T(8,128)S(1)} %get-tuple-element.37, f32[8,768]{1,0:T(8,128)S(1)} %collective-permute-done.15, pred[768]{0:T(1024)(128)(4,1)S(1)} %iota_compare_fusion), kind=kLoop, calls=%fused_computation.4 | loop fusion | flops 18432 | bytes 62208 | tf_op jit(solution)/shard_map/convert_element_type | solution.py:353
  (6 shorter events, 0.1 us)
Async XLA Ops:
  6.1 9.2 %collective-permute-start.2 = (bf16[16,2560]{1,0:T(8,128)(2,1)S(1)}, bf16[16,2560]{1,0:T(8,128)(2,1)S(1)}, u32[]{:S(2)}, u32[]{:S(2)}) collective-permute-start(bf16[16,2560]{1,0:T(8,128)(2,1)S(1)} %get-tuple-element.28), channel_id=1, source_target_pairs={{0,2},{2,0},{4,6},{6,4},{8,10},{10,8},{12,14},{14,12},{16,18},{18,... | collective-permute-start | bytes 245768 | tf_op jit(solution)/shard_map/ppermute | solution.py:28
  9.1 6.2 %collective-permute-start.1 = (bf16[16,2560]{1,0:T(8,128)(2,1)S(1)}, bf16[16,2560]{1,0:T(8,128)(2,1)S(1)}, u32[]{:S(2)}, u32[]{:S(2)}) collective-permute-start(bf16[16,2560]{1,0:T(8,128)(2,1)S(1)} %get-tuple-element.27), channel_id=1, source_target_pairs={{0,4},{2,6},{4,0},{6,2},{8,12},{10,14},{12,8},{14,10},{16,20},{18,... | collective-permute-start | bytes 245768 | tf_op jit(solution)/shard_map/ppermute | solution.py:28
  10.6 5.3 %collective-permute-start = (bf16[16,2560]{1,0:T(8,128)(2,1)S(1)}, bf16[16,2560]{1,0:T(8,128)(2,1)S(1)}, u32[]{:S(2)}, u32[]{:S(2)}) collective-permute-start(bf16[16,2560]{1,0:T(8,128)(2,1)S(1)} %get-tuple-element.26), channel_id=1, source_target_pairs={{0,6},{2,4},{4,2},{6,0},{8,14},{10,12},{12,10},{14,8},{16,22},{18,... | collective-permute-start | bytes 245768 | tf_op jit(solution)/shard_map/ppermute | solution.py:28
  16.0 9.8 %collective-permute-start.5 = (bf16[16,2560]{1,0:T(8,128)(2,1)S(1)}, bf16[16,2560]{1,0:T(8,128)(2,1)S(1)}, u32[]{:S(2)}, u32[]{:S(2)}) collective-permute-start(bf16[16,2560]{1,0:T(8,128)(2,1)S(1)} %get-tuple-element.39), channel_id=1, source_target_pairs={{0,24},{2,26},{4,28},{6,30},{8,16},{10,18},{12,20},{14,22},{16,8},... | collective-permute-start | bytes 245768 | tf_op jit(solution)/shard_map/ppermute | solution.py:28
  19.7 6.2 %collective-permute-start.4 = (bf16[16,2560]{1,0:T(8,128)(2,1)S(1)}, bf16[16,2560]{1,0:T(8,128)(2,1)S(1)}, u32[]{:S(2)}, u32[]{:S(2)}) collective-permute-start(bf16[16,2560]{1,0:T(8,128)(2,1)S(1)} %get-tuple-element.39), channel_id=1, source_target_pairs={{0,16},{2,18},{4,20},{6,22},{8,24},{10,26},{12,28},{14,30},{16,0},... | collective-permute-start | bytes 245768 | tf_op jit(solution)/shard_map/ppermute | solution.py:28
  19.7 6.2 %collective-permute-start.3 = (bf16[16,2560]{1,0:T(8,128)(2,1)S(1)}, bf16[16,2560]{1,0:T(8,128)(2,1)S(1)}, u32[]{:S(2)}, u32[]{:S(2)}) collective-permute-start(bf16[16,2560]{1,0:T(8,128)(2,1)S(1)} %get-tuple-element.39), channel_id=1, source_target_pairs={{0,8},{2,10},{4,12},{6,14},{8,0},{10,2},{12,4},{14,6},{16,24},{18,... | collective-permute-start | bytes 245768 | tf_op jit(solution)/shard_map/ppermute | solution.py:28
  26.0 7.0 %collective-permute-start.6 = (bf16[16,2560]{1,0:T(8,128)(2,1)S(1)}, bf16[16,2560]{1,0:T(8,128)(2,1)S(1)}, u32[]{:S(2)}, u32[]{:S(2)}) collective-permute-start(bf16[16,2560]{1,0:T(8,128)(2,1)S(1)} %add_convert_fusion.fitted_ref), channel_id=1, source_target_pairs={{0,6},{2,4},{4,2},{6,0},{8,14},{10,12},{12,10},{14,8},{16,22},{18,... | collective-permute-start | bytes 245768 | tf_op jit(solution)/shard_map/ppermute | solution.py:28
  28.3 4.6 %collective-permute-start.7 = (bf16[16,2560]{1,0:T(8,128)(2,1)S(1)}, bf16[16,2560]{1,0:T(8,128)(2,1)S(1)}, u32[]{:S(2)}, u32[]{:S(2)}) collective-permute-start(bf16[16,2560]{1,0:T(8,128)(2,1)S(1)} %add_convert_fusion.fitted_ref), channel_id=1, source_target_pairs={{0,4},{2,6},{4,0},{6,2},{8,12},{10,14},{12,8},{14,10},{16,20},{18,... | collective-permute-start | bytes 245768 | tf_op jit(solution)/shard_map/ppermute | solution.py:28
  28.8 4.4 %collective-permute-start.8 = (bf16[16,2560]{1,0:T(8,128)(2,1)S(1)}, bf16[16,2560]{1,0:T(8,128)(2,1)S(1)}, u32[]{:S(2)}, u32[]{:S(2)}) collective-permute-start(bf16[16,2560]{1,0:T(8,128)(2,1)S(1)} %add_convert_fusion.fitted_ref), channel_id=1, source_target_pairs={{0,2},{2,0},{4,6},{6,4},{8,10},{10,8},{12,14},{14,12},{16,18},{18,... | collective-permute-start | bytes 245768 | tf_op jit(solution)/shard_map/ppermute | solution.py:28
  36.5 4.0 %collective-permute-start.10 = (bf16[16,1280]{1,0:T(8,128)(2,1)S(1)}, bf16[16,1280]{1,0:T(8,128)(2,1)S(1)}, u32[]{:S(2)}, u32[]{:S(2)}) collective-permute-start(bf16[16,1280]{1,0:T(8,128)(2,1)S(1)} %convert_element_type.47), channel_id=1, source_target_pairs={{1,16},{3,18},{5,20},{7,22},{9,24},{11,26},{13,28},{15,30},{16,1},... | collective-permute-start | bytes 122888 | tf_op jit(solution)/shard_map/ppermute | solution.py:316
  37.2 5.0 %collective-permute-start.9 = (bf16[16,1280]{1,0:T(8,128)(2,1)S(1)}, bf16[16,1280]{1,0:T(8,128)(2,1)S(1)}, u32[]{:S(2)}, u32[]{:S(2)}) collective-permute-start(bf16[16,1280]{1,0:T(8,128)(2,1)S(1)} %convert_element_type.47), channel_id=1, source_target_pairs={{1,0},{3,2},{5,4},{7,6},{9,8},{11,10},{13,12},{15,14},{16,17},{18,... | collective-permute-start | bytes 122888 | tf_op jit(solution)/shard_map/ppermute | solution.py:316
  42.2 4.1 %collective-permute-start.11 = (bf16[16,1280]{1,0:T(8,128)(2,1)S(1)}, bf16[16,1280]{1,0:T(8,128)(2,1)S(1)}, u32[]{:S(2)}, u32[]{:S(2)}) collective-permute-start(bf16[16,1280]{1,0:T(8,128)(2,1)S(1)} %add_convert_fusion.1), channel_id=1, source_target_pairs={{0,8},{2,10},{4,12},{6,14},{8,0},{10,2},{12,4},{14,6},{16,24},{18,... | collective-permute-start | bytes 122888 | tf_op jit(solution)/shard_map/ppermute | solution.py:28
  46.3 6.0 %collective-permute-start.14 = (bf16[2,16,1280]{2,1,0:T(8,128)(2,1)S(1)}, bf16[2,16,1280]{2,1,0:T(8,128)(2,1)S(1)}, u32[]{:S(2)}, u32[]{:S(2)}) collective-permute-start(bf16[2,16,1280]{2,1,0:T(8,128)(2,1)S(1)} %pad_maximum_fusion.rest_0_), channel_id=1, source_target_pairs={{0,6},{2,4},{4,2},{6,0},{8,14},{10,12},{12,10},{14,8},{16,22},{18,... | collective-permute-start | bytes 245768 | tf_op jit(solution)/shard_map/ppermute | solution.py:28
  48.4 6.0 %collective-permute-start.12 = (bf16[2,16,1280]{2,1,0:T(8,128)(2,1)S(1)}, bf16[2,16,1280]{2,1,0:T(8,128)(2,1)S(1)}, u32[]{:S(2)}, u32[]{:S(2)}) collective-permute-start(bf16[2,16,1280]{2,1,0:T(8,128)(2,1)S(1)} %pad_maximum_fusion.rest_0_), channel_id=1, source_target_pairs={{0,4},{2,6},{4,0},{6,2},{8,12},{10,14},{12,8},{14,10},{16,20},{18,... | collective-permute-start | bytes 245768 | tf_op jit(solution)/shard_map/ppermute | solution.py:28
  48.9 5.5 %collective-permute-start.13 = (bf16[2,16,1280]{2,1,0:T(8,128)(2,1)S(1)}, bf16[2,16,1280]{2,1,0:T(8,128)(2,1)S(1)}, u32[]{:S(2)}, u32[]{:S(2)}) collective-permute-start(bf16[2,16,1280]{2,1,0:T(8,128)(2,1)S(1)} %pad_maximum_fusion.rest_0_), channel_id=1, source_target_pairs={{0,2},{2,0},{4,6},{6,4},{8,10},{10,8},{12,14},{14,12},{16,18},{18,... | collective-permute-start | bytes 245768 | tf_op jit(solution)/shard_map/ppermute | solution.py:28
  57.1 1.2 %collective-permute-start.15 = (f32[8,768]{1,0:T(8,128)S(1)}, f32[8,768]{1,0:T(8,128)S(1)}, u32[]{:S(2)}, u32[]{:S(2)}) collective-permute-start(f32[8,768]{1,0:T(8,128)S(1)} %get-tuple-element.38), channel_id=1, source_target_pairs={{0,1},{1,0},{2,3},{3,2},{4,5},{5,4},{6,7},{7,6},{8,9},{9,8},{10,11... | collective-permute-start | bytes 73736 | tf_op jit(solution)/shard_map/ppermute | solution.py:28

commit v3 on v2

--- a/solution.py
+++ b/solution.py
@@ -44,7 +44,11 @@
     return pl.BlockSpec(memory_space=space)
 
 
-SMEM, VMEM, HBM = pltpu.SMEM, pltpu.VMEM, pltpu.HBM
+VMEM, HBM = pltpu.VMEM, pltpu.HBM
+
+
+def field(info_ref, at):
+    return info_ref[...][0, at]
 
 
 def cost(flops, read):
@@ -80,10 +84,10 @@
     outs, (masked_ref, slots_ref, dens_ref, dens_sem, sems) = rest[: len(picks)], rest[len(picks) :]
     first = pltpu.make_async_copy(dens_hbm, dens_ref, dens_sem)
     first.start()
-    copies = slot_copies(info_ref[0] & len(picks), picks, per, tensor_ref, slots_ref, sems)
+    copies = slot_copies(field(info_ref, 0) & len(picks), picks, per, tensor_ref, slots_ref, sems)
     first.wait()
     dens = dens_ref[...]
-    live = lax.broadcasted_iota(jnp.int32, dens.shape, 1) < info_ref[2]
+    live = lax.broadcasted_iota(jnp.int32, dens.shape, 1) < field(info_ref, 2)
     masked = jnp.where(live, dens.astype(F32), 0.0).astype(BF16)
     masked_ref[...] = masked
     fit_terms(masked, copies, per, slots_ref, outs)
@@ -97,7 +101,7 @@
         functools.partial(fit_others_kernel, picks, per),
         out_shape=[jax.ShapeDtypeStruct((k, per * step), BF16) for _ in picks]
         + [jax.ShapeDtypeStruct((k, rows), BF16), VMEM((half_aux // step, rows, step), BF16)],
-        in_specs=[spec(SMEM), spec(HBM), spec(HBM)],
+        in_specs=[spec(VMEM), spec(HBM), spec(HBM)],
         out_specs=[spec(VMEM) for _ in range(len(picks) + 2)],
         scratch_shapes=[
             VMEM((k, rows), BF16),
@@ -124,7 +128,7 @@
     per, top, info_ref, masked_ref, tensor_ref, metric_ref, before_ref, *rest
 ):
     out_ref, slots_ref, held_ref, sems, row_sems = rest
-    digit = info_ref[0] & top
+    digit = field(info_ref, 0) & top
     copies = slot_copies(digit, [0], per, tensor_ref, slots_ref, sems)
     (rows_in,) = row_copies(digit, [0], metric_ref, [held_ref], row_sems)
     fit_terms(masked_ref[...], copies, per, slots_ref, [out_ref])
@@ -142,7 +146,7 @@
             VMEM(slots.shape, BF16),
             VMEM((depth, width), BF16),
         ],
-        in_specs=[spec(SMEM), spec(VMEM), spec(HBM), spec(HBM), spec(VMEM)],
+        in_specs=[spec(VMEM), spec(VMEM), spec(HBM), spec(HBM), spec(VMEM)],
         out_specs=[spec(VMEM) for _ in range(3)],
         scratch_shapes=[pltpu.SemaphoreType.DMA((per,)), pltpu.SemaphoreType.DMA((1,))],
         input_output_aliases={4: 1},
@@ -153,7 +157,7 @@
 
 def fetch_kernel(picks, top, info_ref, metric_ref, own_ref, *rest):
     *held, same_ref, sems = rest
-    copies = row_copies(info_ref[0] & top, picks, metric_ref, held, sems)
+    copies = row_copies(field(info_ref, 0) & top, picks, metric_ref, held, sems)
     same_ref[...] = own_ref[...]
     for copy in copies:
         copy.wait()
@@ -165,7 +169,7 @@
         functools.partial(fetch_kernel, picks, top),
         out_shape=[VMEM((depth, width), BF16) for _ in picks]
         + [jax.ShapeDtypeStruct(own.shape, own.dtype)],
-        in_specs=[spec(SMEM), spec(HBM), spec(VMEM)],
+        in_specs=[spec(VMEM), spec(HBM), spec(VMEM)],
         out_specs=[spec(VMEM) for _ in range(len(picks) + 1)],
         scratch_shapes=[pltpu.SemaphoreType.DMA((len(picks),))],
         compiler_params=params(0),
@@ -177,7 +181,7 @@
     picks, top, info_ref, metric_ref, fitted_ref, held_ref, out_ref, *rest
 ):
     *late, sems = rest
-    copies = row_copies(info_ref[0] & top, picks, metric_ref, late, sems)
+    copies = row_copies(field(info_ref, 0) & top, picks, metric_ref, late, sems)
     out_ref[...] = jnp.dot(fitted_ref[...], held_ref[...], preferred_element_type=F32)
     for copy in copies:
         copy.wait()
@@ -190,7 +194,7 @@
         functools.partial(solve_own_kernel, picks, top),
         out_shape=[jax.ShapeDtypeStruct((k, width), F32)]
         + [VMEM((depth, width), BF16) for _ in picks],
-        in_specs=[spec(SMEM), spec(HBM), spec(VMEM), spec(VMEM)],
+        in_specs=[spec(VMEM), spec(HBM), spec(VMEM), spec(VMEM)],
         out_specs=[spec(VMEM) for _ in range(len(picks) + 1)],
         scratch_shapes=[pltpu.SemaphoreType.DMA((len(picks),))],
         compiler_params=params(0),
@@ -204,7 +208,7 @@
     for x, rows in zip(fitted, held):
         total += jnp.dot(x[...], rows[...], preferred_element_type=F32)
     out_ref[...] = total
-    home = info_ref[0] >> (low.bit_length()) == info_ref[1]
+    home = field(info_ref, 0) >> (low.bit_length()) == field(info_ref, 1)
     home_ref[...] = jnp.where(home, total, 0.0)
 
 
@@ -215,7 +219,7 @@
     return pl.pallas_call(
         functools.partial(solve_others_kernel, count, low),
         out_shape=[VMEM((k, width), F32) for _ in range(2)],
-        in_specs=[spec(SMEM)] + [spec(VMEM) for _ in range(1 + 2 * count)],
+        in_specs=[spec(VMEM)] + [spec(VMEM) for _ in range(1 + 2 * count)],
         out_specs=[spec(VMEM), spec(VMEM)],
         compiler_params=params(0),
         cost_estimate=cost(2 * k * depth * width * count, count * depth * width * 2),
@@ -239,7 +243,7 @@
     else:
         outs = rest
         total = jnp.zeros((pieces[0].shape[1], slots_ref.shape[1]), F32)
-    line, mine = info_ref[0] & (low - 1), info_ref[0] >> (low.bit_length() - 1)
+    line, mine = field(info_ref, 0) & (low - 1), field(info_ref, 0) >> (low.bit_length() - 1)
     step = slots_ref.shape[2]
     for part, place in zip(pieces, which):
         per = part.shape[2] // step
@@ -254,7 +258,7 @@
                     (((1,), (1,)), ((), ())),
                     preferred_element_type=F32,
                 )
-    split_for_cores(total, 0, info_ref[1], outs)
+    split_for_cores(total, 0, field(info_ref, 1), outs)
 
 
 def back(which, low, info, slots, pieces, begun=None, split=True):
@@ -266,7 +270,7 @@
     return pl.pallas_call(
         functools.partial(back_kernel, which, begun is not None, low),
         out_shape=[jax.ShapeDtypeStruct(shape, F32) for shape in shapes],
-        in_specs=[spec(SMEM), spec(VMEM)] + [spec(VMEM) for _ in pieces + extra],
+        in_specs=[spec(VMEM), spec(VMEM)] + [spec(VMEM) for _ in pieces + extra],
         out_specs=[spec(VMEM) for _ in shapes],
         compiler_params=params(0),
         cost_estimate=cost(2 * k * rows * width * count, count * rows * width * 2),
@@ -280,7 +284,7 @@
     me = lax.axis_index("pairs")
     core = lax.axis_index("aux")
     first, rest = sizes[0], sizes[1:]
-    info = jnp.stack([me.astype(jnp.int32), core.astype(jnp.int32), row_count[0]])
+    info = jnp.stack([me.astype(jnp.int32), core.astype(jnp.int32), row_count[0]]).reshape(1, 3)
     width = half_aux // first
 
     others = list(range(first - 1, 0, -1))

time: 59 us -> 56.9 us (0.964)
  Pallas kernels: 27.9 us -> 24.7 us
  waiting for transfers between devices: 6.95 us -> 8.25 us
    pallas_call x3, Pallas kernels: 6 us -> 4.48 us  [back(): pl.pallas_call(functools.partial(back_kernel, which, begun is not None, l...]
    ppermute x14, waiting for transfers between devices: 5.28 us -> 6.58 us  [swap(): return lax.ppermute(x, axis, [(i, i ^ mask) for i in range(count)])]
  transfers between devices with their start and end apart: 16 -> 16, of which waited for: 8 -> 7; matrix products, arithmetic and copies ran while one was open for 0% -> 0% of each run, Pallas kernels for 28% -> 26%
where the time goes in v3:
time: 56.9 us; the launch traced here: 56.8 us
  Pallas kernels  24.7 us (43%)
  starting transfers between devices  22.2 us (39%)
  waiting for transfers between devices  8.25 us (14%)
  other arithmetic  0.82 us (1%)
  between operations  0.78 us (1%)
    ppermute x14, starting transfers between devices, swap(): return lax.ppermute(x, axis, [(i, i ^ mask) for i in range(count)])  18.4 us
    ppermute x14, waiting for transfers between devices, swap(): return lax.ppermute(x, axis, [(i, i ^ mask) for i in range(count)])  6.58 us
    pallas_call x1, Pallas kernels, fit_others(): pl.pallas_call(functools.partial(fit_others_kernel, picks, per), out_shap...  4.86 us
    pallas_call x1, Pallas kernels, fetch(): pl.pallas_call(functools.partial(fetch_kernel, picks, top), out_shape=[VM...  4.79 us
    pallas_call x3, Pallas kernels, back(): pl.pallas_call(functools.partial(back_kernel, which, begun is not None, l...  4.48 us
    pallas_call x1, Pallas kernels, fit_own(): pl.pallas_call(functools.partial(fit_own_kernel, per, top), out_shape=[ja...  4.3 us
    ppermute x2, starting transfers between devices, send(): lax.ppermute(x, ('pairs', 'aux'), [(p * 2 + c, q * 2 + d) for p, c, q, d...  3.81 us
    pallas_call x1, Pallas kernels, solve_own(): pl.pallas_call(functools.partial(solve_own_kernel, picks, top), out_shape...  3.65 us
  transfers between devices with their start and end apart: 16, of which 7 were waited for; matrix products, arithmetic and copies ran while one was open for 0% of the time, Pallas kernels for 26%

profile of v3, /device:TPU:0, one launch (start us, length us, event | category | flops | bytes accessed | tf_op | source)
XLA Modules:
  0.0 56.8 jit_solution(18006335850947991003)
XLA Ops:
  0.7 0.1 add_bitcast_fusion.info_ref
  0.7 4.9 %shard_map.46 = (bf16[16,2560]{1,0:T(8,128)(2,1)S(1)}, bf16[16,2560]{1,0:T(8,128)(2,1)S(1)}, bf16[16,2560]{1,0:T(8,128)(2,1)S(1)}, bf16[16,768]{1,0:T(8,128)(2,1)S(1)}, bf16[16,768,640]{2,1,0:T(8,128)(2,1)S(1)}) custom-call(s32[1,3]{1,0:T(1,128)S(1)} %add_bitcast_fusion.info_ref, bf16[16,768]{1,0:T(8,128)(2,1)} %dens_hbm.1, bf16[768,10240]{1,0:T(8,128)(2,1)} %tensor_ref.3), custom_call_target="tpu_custom_call" | custom-call | flops 188743680 | bytes 11796480 | tf_op jit(solution)/shard_map/pallas_call | solution.py:100
  5.6 3.0 %collective-permute-start.2 = (bf16[16,2560]{1,0:T(8,128)(2,1)S(1)}, bf16[16,2560]{1,0:T(8,128)(2,1)S(1)}, u32[]{:S(2)}, u32[]{:S(2)}) collective-permute-start(bf16[16,2560]{1,0:T(8,128)(2,1)S(1)} %get-tuple-element.28), channel_id=1, source_target_pairs={{0,2},{2,0},{4,6},{6,4},{8,10},{10,8},{12,14},{14,12},{16,18},{18,... | collective-permute-start | bytes 245768 | tf_op jit(solution)/shard_map/ppermute | solution.py:28
  8.6 1.5 %collective-permute-start.1 = (bf16[16,2560]{1,0:T(8,128)(2,1)S(1)}, bf16[16,2560]{1,0:T(8,128)(2,1)S(1)}, u32[]{:S(2)}, u32[]{:S(2)}) collective-permute-start(bf16[16,2560]{1,0:T(8,128)(2,1)S(1)} %get-tuple-element.27), channel_id=1, source_target_pairs={{0,4},{2,6},{4,0},{6,2},{8,12},{10,14},{12,8},{14,10},{16,20},{18,... | collective-permute-start | bytes 245768 | tf_op jit(solution)/shard_map/ppermute | solution.py:28
  10.1 0.0 collective-permute-start
  10.1 4.3 %shard_map.47 = (f32[16,2560]{1,0:T(8,128)S(1)}, bf16[16,768,640]{2,1,0:T(8,128)(2,1)S(1)}, bf16[2560,1280]{1,0:T(8,128)(2,1)S(1)}) custom-call(s32[1,3]{1,0:T(1,128)S(1)} %add_bitcast_fusion.info_ref, bf16[16,768]{1,0:T(8,128)(2,1)S(1)} %get-tuple-element.22.masked_ref, bf16[768,10240]{1,0:T(8,128)(2,1)} %tensor_ref.3, ...), custom_call_target="tpu_custom_call", output_to_operand_aliasing={{1}: (4, {})} | custom-call | flops 62914560 | bytes 10485760 | tf_op jit(solution)/shard_map/pallas_call | solution.py:142
  14.4 0.0 collective-permute-done.2
  14.5 0.0 collective-permute-done.1
  14.5 1.0 %collective-permute-done = bf16[16,2560]{1,0:T(8,128)(2,1)S(1)} collective-permute-done((bf16[16,2560]{1,0:T(8,128)(2,1)S(1)}, bf16[16,2560]{1,0:T(8,128)(2,1)S(1)}, u32[]{:S(2)}, u32[]{:S(2)}) %collective-permute-start) | collective-permute-done | bytes 81952 | tf_op jit(solution)/shard_map/ppermute | solution.py:28
  15.5 3.7 %collective-permute-start.5 = (bf16[16,2560]{1,0:T(8,128)(2,1)S(1)}, bf16[16,2560]{1,0:T(8,128)(2,1)S(1)}, u32[]{:S(2)}, u32[]{:S(2)}) collective-permute-start(bf16[16,2560]{1,0:T(8,128)(2,1)S(1)} %get-tuple-element.39), channel_id=1, source_target_pairs={{0,24},{2,26},{4,28},{6,30},{8,16},{10,18},{12,20},{14,22},{16,8},... | collective-permute-start | bytes 245768 | tf_op jit(solution)/shard_map/ppermute | solution.py:28
  19.2 0.0 collective-permute-start.4
  19.2 0.8 %collective-permute-start.3 = (bf16[16,2560]{1,0:T(8,128)(2,1)S(1)}, bf16[16,2560]{1,0:T(8,128)(2,1)S(1)}, u32[]{:S(2)}, u32[]{:S(2)}) collective-permute-start(bf16[16,2560]{1,0:T(8,128)(2,1)S(1)} %get-tuple-element.39), channel_id=1, source_target_pairs={{0,8},{2,10},{4,12},{6,14},{8,0},{10,2},{12,4},{14,6},{16,24},{18,... | collective-permute-start | bytes 245768 | tf_op jit(solution)/shard_map/ppermute | solution.py:28
  20.0 4.8 %shard_map.48 = (bf16[2560,1280]{1,0:T(8,128)(2,1)S(1)}, bf16[2560,1280]{1,0:T(8,128)(2,1)S(1)}, f32[16,2560]{1,0:T(8,128)S(1)}) custom-call(s32[1,3]{1,0:T(1,128)S(1)} %add_bitcast_fusion.info_ref, bf16[10240,1280]{1,0:T(8,128)(2,1)} %metric_ref.5, f32[16,2560]{1,0:T(8,128)S(1)} %get-tuple-element.40.own_ref), custom_call_target="tpu_custom_call" | custom-call | bytes 13107200 | tf_op jit(solution)/shard_map/pallas_call | solution.py:168
  24.8 0.0 collective-permute-done.5
  24.8 0.3 collective-permute-done.4
  25.1 0.0 collective-permute-done.3
  25.2 2.4 %collective-permute-start.6 = (bf16[16,2560]{1,0:T(8,128)(2,1)S(1)}, bf16[16,2560]{1,0:T(8,128)(2,1)S(1)}, u32[]{:S(2)}, u32[]{:S(2)}) collective-permute-start(bf16[16,2560]{1,0:T(8,128)(2,1)S(1)} %add_convert_fusion.fitted_ref), channel_id=1, source_target_pairs={{0,6},{2,4},{4,2},{6,0},{8,14},{10,12},{12,10},{14,8},{16,22},{18,... | collective-permute-start | bytes 245768 | tf_op jit(solution)/shard_map/ppermute | solution.py:28
  27.5 0.4 collective-permute-start.7
  28.0 0.8 %collective-permute-start.8 = (bf16[16,2560]{1,0:T(8,128)(2,1)S(1)}, bf16[16,2560]{1,0:T(8,128)(2,1)S(1)}, u32[]{:S(2)}, u32[]{:S(2)}) collective-permute-start(bf16[16,2560]{1,0:T(8,128)(2,1)S(1)} %add_convert_fusion.fitted_ref), channel_id=1, source_target_pairs={{0,2},{2,0},{4,6},{6,4},{8,10},{10,8},{12,14},{14,12},{16,18},{18,... | collective-permute-start | bytes 245768 | tf_op jit(solution)/shard_map/ppermute | solution.py:28
  28.7 3.7 %shard_map.49 = (f32[16,1280]{1,0:T(8,128)S(1)}, bf16[2560,1280]{1,0:T(8,128)(2,1)S(1)}) custom-call(s32[1,3]{1,0:T(1,128)S(1)} %add_bitcast_fusion.info_ref, bf16[10240,1280]{1,0:T(8,128)(2,1)} %metric_ref.5, bf16[16,2560]{1,0:T(8,128)(2,1)S(1)} %add_convert_fusion.fitted_ref, bf16[2560,1280]{1,0:T(8,128)(2,1)S(1)} %get-tuple-element.30.held_ref), custom_call_target="tpu_custom_call" | custom-call | flops 104857600 | bytes 13107200 | tf_op jit(solution)/shard_map/pallas_call | solution.py:193
  32.4 0.0 collective-permute-done.6.rest_0_
  32.4 0.0 collective-permute-done.7.rest_1_
  32.4 0.0 collective-permute-done.8.rest_2_
  32.4 2.7 %shard_map.50 = (f32[16,1280]{1,0:T(8,128)S(1)}, f32[16,1280]{1,0:T(8,128)S(1)}) custom-call(s32[1,3]{1,0:T(1,128)S(1)} %add_bitcast_fusion.info_ref, f32[16,1280]{1,0:T(8,128)S(1)} %get-tuple-element.31.begun_ref, bf16[16,2560]{1,0:T(8,128)(2,1)S(1)} %collective-permute-done.6.rest_0_, bf16[16,2560]{1,0:T(8,128)(2,1)S(1)} %collective-permute-done.7.rest_1_, ...), custom_call_target="tpu_custom_call" | custom-call | flops 314572800 | bytes 19660800 | tf_op jit(solution)/shard_map/pallas_call | solution.py:219
  35.1 0.7 %collective-permute-start.10 = (bf16[16,1280]{1,0:T(8,128)(2,1)S(1)}, bf16[16,1280]{1,0:T(8,128)(2,1)S(1)}, u32[]{:S(2)}, u32[]{:S(2)}) collective-permute-start(bf16[16,1280]{1,0:T(8,128)(2,1)S(1)} %convert_element_type.47), channel_id=1, source_target_pairs={{1,16},{3,18},{5,20},{7,22},{9,24},{11,26},{13,28},{15,30},{16,1},... | collective-permute-start | bytes 122888 | tf_op jit(solution)/shard_map/ppermute | solution.py:320
  35.8 3.1 %collective-permute-start.9 = (bf16[16,1280]{1,0:T(8,128)(2,1)S(1)}, bf16[16,1280]{1,0:T(8,128)(2,1)S(1)}, u32[]{:S(2)}, u32[]{:S(2)}) collective-permute-start(bf16[16,1280]{1,0:T(8,128)(2,1)S(1)} %convert_element_type.47), channel_id=1, source_target_pairs={{1,0},{3,2},{5,4},{7,6},{9,8},{11,10},{13,12},{15,14},{16,17},{18,... | collective-permute-start | bytes 122888 | tf_op jit(solution)/shard_map/ppermute | solution.py:320
  38.9 0.0 collective-permute-done.10
  38.9 1.7 %collective-permute-done.9 = bf16[16,1280]{1,0:T(8,128)(2,1)S(1)} collective-permute-done((bf16[16,1280]{1,0:T(8,128)(2,1)S(1)}, bf16[16,1280]{1,0:T(8,128)(2,1)S(1)}, u32[]{:S(2)}, u32[]{:S(2)}) %collective-permute-start.9) | collective-permute-done | bytes 40992 | tf_op jit(solution)/shard_map/ppermute | solution.py:320
  40.6 2.1 %collective-permute-start.11 = (bf16[16,1280]{1,0:T(8,128)(2,1)S(1)}, bf16[16,1280]{1,0:T(8,128)(2,1)S(1)}, u32[]{:S(2)}, u32[]{:S(2)}) collective-permute-start(bf16[16,1280]{1,0:T(8,128)(2,1)S(1)} %add_convert_fusion.1), channel_id=1, source_target_pairs={{0,8},{2,10},{4,12},{6,14},{8,0},{10,2},{12,4},{14,6},{16,24},{18,... | collective-permute-start | bytes 122888 | tf_op jit(solution)/shard_map/ppermute | solution.py:28
  42.7 2.0 %collective-permute-done.11 = bf16[16,1280]{1,0:T(8,128)(2,1)S(1)} collective-permute-done((bf16[16,1280]{1,0:T(8,128)(2,1)S(1)}, bf16[16,1280]{1,0:T(8,128)(2,1)S(1)}, u32[]{:S(2)}, u32[]{:S(2)}) %collective-permute-start.11) | collective-permute-done | bytes 40992 | tf_op jit(solution)/shard_map/ppermute | solution.py:28
  44.7 2.1 %collective-permute-start.14 = (bf16[2,16,1280]{2,1,0:T(8,128)(2,1)S(1)}, bf16[2,16,1280]{2,1,0:T(8,128)(2,1)S(1)}, u32[]{:S(2)}, u32[]{:S(2)}) collective-permute-start(bf16[2,16,1280]{2,1,0:T(8,128)(2,1)S(1)} %pad_maximum_fusion.rest_0_), channel_id=1, source_target_pairs={{0,6},{2,4},{4,2},{6,0},{8,14},{10,12},{12,10},{14,8},{16,22},{18,... | collective-permute-start | bytes 245768 | tf_op jit(solution)/shard_map/ppermute | solution.py:28
  46.8 0.4 collective-permute-start.12
  47.2 1.1 %collective-permute-start.13 = (bf16[2,16,1280]{2,1,0:T(8,128)(2,1)S(1)}, bf16[2,16,1280]{2,1,0:T(8,128)(2,1)S(1)}, u32[]{:S(2)}, u32[]{:S(2)}) collective-permute-start(bf16[2,16,1280]{2,1,0:T(8,128)(2,1)S(1)} %pad_maximum_fusion.rest_0_), channel_id=1, source_target_pairs={{0,2},{2,0},{4,6},{6,4},{8,10},{10,8},{12,14},{14,12},{16,18},{18,... | collective-permute-start | bytes 245768 | tf_op jit(solution)/shard_map/ppermute | solution.py:28
  48.3 1.2 %shard_map.51.rest_1_ = f32[16,768]{1,0:T(8,128)S(1)} custom-call(s32[1,3]{1,0:T(1,128)S(1)} %add_bitcast_fusion.info_ref, bf16[16,768,640]{2,1,0:T(8,128)(2,1)S(1)} %get-tuple-element.24.slots_ref, bf16[2,16,1280]{2,1,0:T(8,128)(2,1)S(1)} %pad_maximum_fusion.rest_0_), custom_call_target="tpu_custom_call" | custom-call | flops 62914560 | bytes 3932160 | tf_op jit(solution)/shard_map/pallas_call | solution.py:270
  49.4 1.3 %collective-permute-done.14.rest_0_ = bf16[2,16,1280]{2,1,0:T(8,128)(2,1)S(1)} collective-permute-done((bf16[2,16,1280]{2,1,0:T(8,128)(2,1)S(1)}, bf16[2,16,1280]{2,1,0:T(8,128)(2,1)S(1)}, u32[]{:S(2)}, u32[]{:S(2)}) %collective-permute-start.14) | collective-permute-done | bytes 81952 | tf_op jit(solution)/shard_map/ppermute | solution.py:28
  50.8 1.2 %shard_map.52.rest_2_ = f32[16,768]{1,0:T(8,128)S(1)} custom-call(s32[1,3]{1,0:T(1,128)S(1)} %add_bitcast_fusion.info_ref, bf16[16,768,640]{2,1,0:T(8,128)(2,1)S(1)} %get-tuple-element.24.slots_ref, bf16[2,16,1280]{2,1,0:T(8,128)(2,1)S(1)} %collective-permute-done.14.rest_0_, f32[16,768]{1,0:T(8,128)S(1)} %shard_map.51.rest_1_), custom_call_target="tpu_custom_call" | custom-call | flops 62914560 | bytes 3932160 | tf_op jit(solution)/shard_map/pallas_call | solution.py:270
  51.9 0.9 %collective-permute-done.12.rest_0_ = bf16[2,16,1280]{2,1,0:T(8,128)(2,1)S(1)} collective-permute-done((bf16[2,16,1280]{2,1,0:T(8,128)(2,1)S(1)}, bf16[2,16,1280]{2,1,0:T(8,128)(2,1)S(1)}, u32[]{:S(2)}, u32[]{:S(2)}) %collective-permute-start.12) | collective-permute-done | bytes 81952 | tf_op jit(solution)/shard_map/ppermute | solution.py:28
  52.8 0.0 collective-permute-done.13.rest_1_
  52.8 2.2 %shard_map.53 = (f32[8,768]{1,0:T(8,128)S(1)}, f32[8,768]{1,0:T(8,128)S(1)}) custom-call(s32[1,3]{1,0:T(1,128)S(1)} %add_bitcast_fusion.info_ref, bf16[16,768,640]{2,1,0:T(8,128)(2,1)S(1)} %get-tuple-element.24.slots_ref, bf16[2,16,1280]{2,1,0:T(8,128)(2,1)S(1)} %collective-permute-done.12.rest_0_, bf16[2,16,1280]{2,1,0:T(8,128)(2,1)S(1)} %collective-permute-done.13.rest_1_, ...), custom_call_target="tpu_custom_call" | custom-call | flops 125829120 | bytes 7864320 | tf_op jit(solution)/shard_map/pallas_call | solution.py:270
  54.9 0.1 collective-permute-start.15
  55.1 1.1 %collective-permute-done.15 = f32[8,768]{1,0:T(8,128)S(1)} collective-permute-done((f32[8,768]{1,0:T(8,128)S(1)}, f32[8,768]{1,0:T(8,128)S(1)}, u32[]{:S(2)}, u32[]{:S(2)}) %collective-permute-start.15) | collective-permute-done | bytes 24608 | tf_op jit(solution)/shard_map/ppermute | solution.py:28
  56.2 0.6 %select_convert_fusion = bf16[8,768]{1,0:T(8,128)(2,1)} fusion(f32[8,768]{1,0:T(8,128)S(1)} %get-tuple-element.37, f32[8,768]{1,0:T(8,128)S(1)} %collective-permute-done.15, pred[768]{0:T(1024)(128)(4,1)S(1)} %iota_compare_fusion), kind=kLoop, calls=%fused_computation.4 | loop fusion | flops 18432 | bytes 62208 | tf_op jit(solution)/shard_map/convert_element_type | solution.py:357
  (6 shorter events, 0.1 us)
Async XLA Ops:
  5.6 8.9 %collective-permute-start.2 = (bf16[16,2560]{1,0:T(8,128)(2,1)S(1)}, bf16[16,2560]{1,0:T(8,128)(2,1)S(1)}, u32[]{:S(2)}, u32[]{:S(2)}) collective-permute-start(bf16[16,2560]{1,0:T(8,128)(2,1)S(1)} %get-tuple-element.28), channel_id=1, source_target_pairs={{0,2},{2,0},{4,6},{6,4},{8,10},{10,8},{12,14},{14,12},{16,18},{18,... | collective-permute-start | bytes 245768 | tf_op jit(solution)/shard_map/ppermute | solution.py:28
  8.6 5.9 %collective-permute-start.1 = (bf16[16,2560]{1,0:T(8,128)(2,1)S(1)}, bf16[16,2560]{1,0:T(8,128)(2,1)S(1)}, u32[]{:S(2)}, u32[]{:S(2)}) collective-permute-start(bf16[16,2560]{1,0:T(8,128)(2,1)S(1)} %get-tuple-element.27), channel_id=1, source_target_pairs={{0,4},{2,6},{4,0},{6,2},{8,12},{10,14},{12,8},{14,10},{16,20},{18,... | collective-permute-start | bytes 245768 | tf_op jit(solution)/shard_map/ppermute | solution.py:28
  10.1 5.3 %collective-permute-start = (bf16[16,2560]{1,0:T(8,128)(2,1)S(1)}, bf16[16,2560]{1,0:T(8,128)(2,1)S(1)}, u32[]{:S(2)}, u32[]{:S(2)}) collective-permute-start(bf16[16,2560]{1,0:T(8,128)(2,1)S(1)} %get-tuple-element.26), channel_id=1, source_target_pairs={{0,6},{2,4},{4,2},{6,0},{8,14},{10,12},{12,10},{14,8},{16,22},{18,... | collective-permute-start | bytes 245768 | tf_op jit(solution)/shard_map/ppermute | solution.py:28
  15.5 9.3 %collective-permute-start.5 = (bf16[16,2560]{1,0:T(8,128)(2,1)S(1)}, bf16[16,2560]{1,0:T(8,128)(2,1)S(1)}, u32[]{:S(2)}, u32[]{:S(2)}) collective-permute-start(bf16[16,2560]{1,0:T(8,128)(2,1)S(1)} %get-tuple-element.39), channel_id=1, source_target_pairs={{0,24},{2,26},{4,28},{6,30},{8,16},{10,18},{12,20},{14,22},{16,8},... | collective-permute-start | bytes 245768 | tf_op jit(solution)/shard_map/ppermute | solution.py:28
  19.2 5.9 %collective-permute-start.4 = (bf16[16,2560]{1,0:T(8,128)(2,1)S(1)}, bf16[16,2560]{1,0:T(8,128)(2,1)S(1)}, u32[]{:S(2)}, u32[]{:S(2)}) collective-permute-start(bf16[16,2560]{1,0:T(8,128)(2,1)S(1)} %get-tuple-element.39), channel_id=1, source_target_pairs={{0,16},{2,18},{4,20},{6,22},{8,24},{10,26},{12,28},{14,30},{16,0},... | collective-permute-start | bytes 245768 | tf_op jit(solution)/shard_map/ppermute | solution.py:28
  19.2 5.9 %collective-permute-start.3 = (bf16[16,2560]{1,0:T(8,128)(2,1)S(1)}, bf16[16,2560]{1,0:T(8,128)(2,1)S(1)}, u32[]{:S(2)}, u32[]{:S(2)}) collective-permute-start(bf16[16,2560]{1,0:T(8,128)(2,1)S(1)} %get-tuple-element.39), channel_id=1, source_target_pairs={{0,8},{2,10},{4,12},{6,14},{8,0},{10,2},{12,4},{14,6},{16,24},{18,... | collective-permute-start | bytes 245768 | tf_op jit(solution)/shard_map/ppermute | solution.py:28
  25.2 7.2 %collective-permute-start.6 = (bf16[16,2560]{1,0:T(8,128)(2,1)S(1)}, bf16[16,2560]{1,0:T(8,128)(2,1)S(1)}, u32[]{:S(2)}, u32[]{:S(2)}) collective-permute-start(bf16[16,2560]{1,0:T(8,128)(2,1)S(1)} %add_convert_fusion.fitted_ref), channel_id=1, source_target_pairs={{0,6},{2,4},{4,2},{6,0},{8,14},{10,12},{12,10},{14,8},{16,22},{18,... | collective-permute-start | bytes 245768 | tf_op jit(solution)/shard_map/ppermute | solution.py:28
  27.5 4.9 %collective-permute-start.7 = (bf16[16,2560]{1,0:T(8,128)(2,1)S(1)}, bf16[16,2560]{1,0:T(8,128)(2,1)S(1)}, u32[]{:S(2)}, u32[]{:S(2)}) collective-permute-start(bf16[16,2560]{1,0:T(8,128)(2,1)S(1)} %add_convert_fusion.fitted_ref), channel_id=1, source_target_pairs={{0,4},{2,6},{4,0},{6,2},{8,12},{10,14},{12,8},{14,10},{16,20},{18,... | collective-permute-start | bytes 245768 | tf_op jit(solution)/shard_map/ppermute | solution.py:28
  28.0 4.4 %collective-permute-start.8 = (bf16[16,2560]{1,0:T(8,128)(2,1)S(1)}, bf16[16,2560]{1,0:T(8,128)(2,1)S(1)}, u32[]{:S(2)}, u32[]{:S(2)}) collective-permute-start(bf16[16,2560]{1,0:T(8,128)(2,1)S(1)} %add_convert_fusion.fitted_ref), channel_id=1, source_target_pairs={{0,2},{2,0},{4,6},{6,4},{8,10},{10,8},{12,14},{14,12},{16,18},{18,... | collective-permute-start | bytes 245768 | tf_op jit(solution)/shard_map/ppermute | solution.py:28
  35.1 3.8 %collective-permute-start.10 = (bf16[16,1280]{1,0:T(8,128)(2,1)S(1)}, bf16[16,1280]{1,0:T(8,128)(2,1)S(1)}, u32[]{:S(2)}, u32[]{:S(2)}) collective-permute-start(bf16[16,1280]{1,0:T(8,128)(2,1)S(1)} %convert_element_type.47), channel_id=1, source_target_pairs={{1,16},{3,18},{5,20},{7,22},{9,24},{11,26},{13,28},{15,30},{16,1},... | collective-permute-start | bytes 122888 | tf_op jit(solution)/shard_map/ppermute | solution.py:320
  35.8 4.8 %collective-permute-start.9 = (bf16[16,1280]{1,0:T(8,128)(2,1)S(1)}, bf16[16,1280]{1,0:T(8,128)(2,1)S(1)}, u32[]{:S(2)}, u32[]{:S(2)}) collective-permute-start(bf16[16,1280]{1,0:T(8,128)(2,1)S(1)} %convert_element_type.47), channel_id=1, source_target_pairs={{1,0},{3,2},{5,4},{7,6},{9,8},{11,10},{13,12},{15,14},{16,17},{18,... | collective-permute-start | bytes 122888 | tf_op jit(solution)/shard_map/ppermute | solution.py:320
  40.6 4.1 %collective-permute-start.11 = (bf16[16,1280]{1,0:T(8,128)(2,1)S(1)}, bf16[16,1280]{1,0:T(8,128)(2,1)S(1)}, u32[]{:S(2)}, u32[]{:S(2)}) collective-permute-start(bf16[16,1280]{1,0:T(8,128)(2,1)S(1)} %add_convert_fusion.1), channel_id=1, source_target_pairs={{0,8},{2,10},{4,12},{6,14},{8,0},{10,2},{12,4},{14,6},{16,24},{18,... | collective-permute-start | bytes 122888 | tf_op jit(solution)/shard_map/ppermute | solution.py:28
  44.7 6.0 %collective-permute-start.14 = (bf16[2,16,1280]{2,1,0:T(8,128)(2,1)S(1)}, bf16[2,16,1280]{2,1,0:T(8,128)(2,1)S(1)}, u32[]{:S(2)}, u32[]{:S(2)}) collective-permute-start(bf16[2,16,1280]{2,1,0:T(8,128)(2,1)S(1)} %pad_maximum_fusion.rest_0_), channel_id=1, source_target_pairs={{0,6},{2,4},{4,2},{6,0},{8,14},{10,12},{12,10},{14,8},{16,22},{18,... | collective-permute-start | bytes 245768 | tf_op jit(solution)/shard_map/ppermute | solution.py:28
  46.8 6.0 %collective-permute-start.12 = (bf16[2,16,1280]{2,1,0:T(8,128)(2,1)S(1)}, bf16[2,16,1280]{2,1,0:T(8,128)(2,1)S(1)}, u32[]{:S(2)}, u32[]{:S(2)}) collective-permute-start(bf16[2,16,1280]{2,1,0:T(8,128)(2,1)S(1)} %pad_maximum_fusion.rest_0_), channel_id=1, source_target_pairs={{0,4},{2,6},{4,0},{6,2},{8,12},{10,14},{12,8},{14,10},{16,20},{18,... | collective-permute-start | bytes 245768 | tf_op jit(solution)/shard_map/ppermute | solution.py:28
  47.2 5.5 %collective-permute-start.13 = (bf16[2,16,1280]{2,1,0:T(8,128)(2,1)S(1)}, bf16[2,16,1280]{2,1,0:T(8,128)(2,1)S(1)}, u32[]{:S(2)}, u32[]{:S(2)}) collective-permute-start(bf16[2,16,1280]{2,1,0:T(8,128)(2,1)S(1)} %pad_maximum_fusion.rest_0_), channel_id=1, source_target_pairs={{0,2},{2,0},{4,6},{6,4},{8,10},{10,8},{12,14},{14,12},{16,18},{18,... | collective-permute-start | bytes 245768 | tf_op jit(solution)/shard_map/ppermute | solution.py:28
  54.9 1.2 %collective-permute-start.15 = (f32[8,768]{1,0:T(8,128)S(1)}, f32[8,768]{1,0:T(8,128)S(1)}, u32[]{:S(2)}, u32[]{:S(2)}) collective-permute-start(f32[8,768]{1,0:T(8,128)S(1)} %get-tuple-element.38), channel_id=1, source_target_pairs={{0,1},{1,0},{2,3},{3,2},{4,5},{5,4},{6,7},{7,6},{8,9},{9,8},{10,11... | collective-permute-start | bytes 73736 | tf_op jit(solution)/shard_map/ppermute | solution.py:28

commit v4 on v3

--- a/solution.py
+++ b/solution.py
@@ -321,9 +321,9 @@
 
     term = part.astype(BF16)
     first_pairs = [(p, 1 - c, p, c) for p, c in homes] + [(p, c, p ^ across, c) for p, c in homes]
+    third_term = send(term, [(p, 1 - c, p ^ across, c) for p, c in homes])
     other_term = send(term, first_pairs)
-    third_term = send(term, [(p, 1 - c, p ^ across, c) for p, c in homes])
-    own = (at_home + other_term.astype(F32) + third_term.astype(F32)).astype(BF16)
+    own = (at_home + third_term.astype(F32) + other_term.astype(F32)).astype(BF16)
     line_blocks = jnp.stack([own, swap(own, "pairs", n_pairs, low)])
 
     if block % step == 0 and len(sizes) == 2:

time: 56.9 us -> 55.3 us (0.972)
  waiting for transfers between devices: 8.25 us -> 7.39 us
  starting transfers between devices: 22.2 us -> 21.4 us
    ppermute x2, starting transfers between devices: 3.81 us -> 2.54 us  [send(): lax.ppermute(x, ('pairs', 'aux'), [(p * 2 + c, q * 2 + d) for p, c, q, d...]
    ppermute x2, waiting for transfers between devices: 1.67 us -> 1.02 us  [send(): lax.ppermute(x, ('pairs', 'aux'), [(p * 2 + c, q * 2 + d) for p, c, q, d...]
  transfers between devices with their start and end apart: 16 -> 16, of which waited for: 7 -> 8; matrix products, arithmetic and copies ran while one was open for 0% -> 0% of each run, Pallas kernels for 26% -> 27%
where the time goes in v4:
time: 55.3 us; the launch traced here: 55.2 us
  Pallas kernels  24.7 us (45%)
  starting transfers between devices  21.4 us (39%)
  waiting for transfers between devices  7.39 us (13%)
  other arithmetic  0.82 us (1%)
  between operations  0.78 us (1%)
    ppermute x14, starting transfers between devices, swap(): return lax.ppermute(x, axis, [(i, i ^ mask) for i in range(count)])  18.9 us
    ppermute x14, waiting for transfers between devices, swap(): return lax.ppermute(x, axis, [(i, i ^ mask) for i in range(count)])  6.37 us
    pallas_call x1, Pallas kernels, fit_others(): pl.pallas_call(functools.partial(fit_others_kernel, picks, per), out_shap...  4.86 us
    pallas_call x1, Pallas kernels, fetch(): pl.pallas_call(functools.partial(fetch_kernel, picks, top), out_shape=[VM...  4.79 us
    pallas_call x3, Pallas kernels, back(): pl.pallas_call(functools.partial(back_kernel, which, begun is not None, l...  4.48 us
    pallas_call x1, Pallas kernels, fit_own(): pl.pallas_call(functools.partial(fit_own_kernel, per, top), out_shape=[ja...  4.3 us
    pallas_call x1, Pallas kernels, solve_own(): pl.pallas_call(functools.partial(solve_own_kernel, picks, top), out_shape...  3.65 us
    pallas_call x1, Pallas kernels, solve_others(): pl.pallas_call(functools.partial(solve_others_kernel, count, low), out_sh...  2.65 us
  transfers between devices with their start and end apart: 16, of which 8 were waited for; matrix products, arithmetic and copies ran while one was open for 0% of the time, Pallas kernels for 27%

profile of v4, /device:TPU:0, one launch (start us, length us, event | category | flops | bytes accessed | tf_op | source)
XLA Modules:
  0.0 55.2 jit_solution(595572187484027682)
XLA Ops:
  0.7 0.1 add_bitcast_fusion.info_ref
  0.7 4.9 %shard_map.46 = (bf16[16,2560]{1,0:T(8,128)(2,1)S(1)}, bf16[16,2560]{1,0:T(8,128)(2,1)S(1)}, bf16[16,2560]{1,0:T(8,128)(2,1)S(1)}, bf16[16,768]{1,0:T(8,128)(2,1)S(1)}, bf16[16,768,640]{2,1,0:T(8,128)(2,1)S(1)}) custom-call(s32[1,3]{1,0:T(1,128)S(1)} %add_bitcast_fusion.info_ref, bf16[16,768]{1,0:T(8,128)(2,1)} %dens_hbm.1, bf16[768,10240]{1,0:T(8,128)(2,1)} %tensor_ref.3), custom_call_target="tpu_custom_call" | custom-call | flops 188743680 | bytes 11796480 | tf_op jit(solution)/shard_map/pallas_call | solution.py:100
  5.6 3.0 %collective-permute-start.2 = (bf16[16,2560]{1,0:T(8,128)(2,1)S(1)}, bf16[16,2560]{1,0:T(8,128)(2,1)S(1)}, u32[]{:S(2)}, u32[]{:S(2)}) collective-permute-start(bf16[16,2560]{1,0:T(8,128)(2,1)S(1)} %get-tuple-element.28), channel_id=1, source_target_pairs={{0,2},{2,0},{4,6},{6,4},{8,10},{10,8},{12,14},{14,12},{16,18},{18,... | collective-permute-start | bytes 245768 | tf_op jit(solution)/shard_map/ppermute | solution.py:28
  8.6 1.5 %collective-permute-start.1 = (bf16[16,2560]{1,0:T(8,128)(2,1)S(1)}, bf16[16,2560]{1,0:T(8,128)(2,1)S(1)}, u32[]{:S(2)}, u32[]{:S(2)}) collective-permute-start(bf16[16,2560]{1,0:T(8,128)(2,1)S(1)} %get-tuple-element.27), channel_id=1, source_target_pairs={{0,4},{2,6},{4,0},{6,2},{8,12},{10,14},{12,8},{14,10},{16,20},{18,... | collective-permute-start | bytes 245768 | tf_op jit(solution)/shard_map/ppermute | solution.py:28
  10.1 0.0 collective-permute-start
  10.1 4.3 %shard_map.47 = (f32[16,2560]{1,0:T(8,128)S(1)}, bf16[16,768,640]{2,1,0:T(8,128)(2,1)S(1)}, bf16[2560,1280]{1,0:T(8,128)(2,1)S(1)}) custom-call(s32[1,3]{1,0:T(1,128)S(1)} %add_bitcast_fusion.info_ref, bf16[16,768]{1,0:T(8,128)(2,1)S(1)} %get-tuple-element.22.masked_ref, bf16[768,10240]{1,0:T(8,128)(2,1)} %tensor_ref.3, ...), custom_call_target="tpu_custom_call", output_to_operand_aliasing={{1}: (4, {})} | custom-call | flops 62914560 | bytes 10485760 | tf_op jit(solution)/shard_map/pallas_call | solution.py:142
  14.4 0.0 collective-permute-done.2
  14.5 0.0 collective-permute-done.1
  14.5 1.0 %collective-permute-done = bf16[16,2560]{1,0:T(8,128)(2,1)S(1)} collective-permute-done((bf16[16,2560]{1,0:T(8,128)(2,1)S(1)}, bf16[16,2560]{1,0:T(8,128)(2,1)S(1)}, u32[]{:S(2)}, u32[]{:S(2)}) %collective-permute-start) | collective-permute-done | bytes 81952 | tf_op jit(solution)/shard_map/ppermute | solution.py:28
  15.5 3.7 %collective-permute-start.5 = (bf16[16,2560]{1,0:T(8,128)(2,1)S(1)}, bf16[16,2560]{1,0:T(8,128)(2,1)S(1)}, u32[]{:S(2)}, u32[]{:S(2)}) collective-permute-start(bf16[16,2560]{1,0:T(8,128)(2,1)S(1)} %get-tuple-element.39), channel_id=1, source_target_pairs={{0,24},{2,26},{4,28},{6,30},{8,16},{10,18},{12,20},{14,22},{16,8},... | collective-permute-start | bytes 245768 | tf_op jit(solution)/shard_map/ppermute | solution.py:28
  19.2 0.0 collective-permute-start.4
  19.2 0.8 %collective-permute-start.3 = (bf16[16,2560]{1,0:T(8,128)(2,1)S(1)}, bf16[16,2560]{1,0:T(8,128)(2,1)S(1)}, u32[]{:S(2)}, u32[]{:S(2)}) collective-permute-start(bf16[16,2560]{1,0:T(8,128)(2,1)S(1)} %get-tuple-element.39), channel_id=1, source_target_pairs={{0,8},{2,10},{4,12},{6,14},{8,0},{10,2},{12,4},{14,6},{16,24},{18,... | collective-permute-start | bytes 245768 | tf_op jit(solution)/shard_map/ppermute | solution.py:28
  20.0 4.8 %shard_map.48 = (bf16[2560,1280]{1,0:T(8,128)(2,1)S(1)}, bf16[2560,1280]{1,0:T(8,128)(2,1)S(1)}, f32[16,2560]{1,0:T(8,128)S(1)}) custom-call(s32[1,3]{1,0:T(1,128)S(1)} %add_bitcast_fusion.info_ref, bf16[10240,1280]{1,0:T(8,128)(2,1)} %metric_ref.5, f32[16,2560]{1,0:T(8,128)S(1)} %get-tuple-element.40.own_ref), custom_call_target="tpu_custom_call" | custom-call | bytes 13107200 | tf_op jit(solution)/shard_map/pallas_call | solution.py:168
  24.8 0.0 collective-permute-done.5
  24.8 0.3 collective-permute-done.4
  25.1 0.0 collective-permute-done.3
  25.2 2.4 %collective-permute-start.6 = (bf16[16,2560]{1,0:T(8,128)(2,1)S(1)}, bf16[16,2560]{1,0:T(8,128)(2,1)S(1)}, u32[]{:S(2)}, u32[]{:S(2)}) collective-permute-start(bf16[16,2560]{1,0:T(8,128)(2,1)S(1)} %add_convert_fusion.fitted_ref), channel_id=1, source_target_pairs={{0,6},{2,4},{4,2},{6,0},{8,14},{10,12},{12,10},{14,8},{16,22},{18,... | collective-permute-start | bytes 245768 | tf_op jit(solution)/shard_map/ppermute | solution.py:28
  27.5 0.4 collective-permute-start.7
  28.0 0.8 %collective-permute-start.8 = (bf16[16,2560]{1,0:T(8,128)(2,1)S(1)}, bf16[16,2560]{1,0:T(8,128)(2,1)S(1)}, u32[]{:S(2)}, u32[]{:S(2)}) collective-permute-start(bf16[16,2560]{1,0:T(8,128)(2,1)S(1)} %add_convert_fusion.fitted_ref), channel_id=1, source_target_pairs={{0,2},{2,0},{4,6},{6,4},{8,10},{10,8},{12,14},{14,12},{16,18},{18,... | collective-permute-start | bytes 245768 | tf_op jit(solution)/shard_map/ppermute | solution.py:28
  28.7 3.7 %shard_map.49 = (f32[16,1280]{1,0:T(8,128)S(1)}, bf16[2560,1280]{1,0:T(8,128)(2,1)S(1)}) custom-call(s32[1,3]{1,0:T(1,128)S(1)} %add_bitcast_fusion.info_ref, bf16[10240,1280]{1,0:T(8,128)(2,1)} %metric_ref.5, bf16[16,2560]{1,0:T(8,128)(2,1)S(1)} %add_convert_fusion.fitted_ref, bf16[2560,1280]{1,0:T(8,128)(2,1)S(1)} %get-tuple-element.30.held_ref), custom_call_target="tpu_custom_call" | custom-call | flops 104857600 | bytes 13107200 | tf_op jit(solution)/shard_map/pallas_call | solution.py:193
  32.4 0.0 collective-permute-done.6.rest_0_
  32.4 0.0 collective-permute-done.7.rest_1_
  32.4 0.0 collective-permute-done.8.rest_2_
  32.4 2.7 %shard_map.50 = (f32[16,1280]{1,0:T(8,128)S(1)}, f32[16,1280]{1,0:T(8,128)S(1)}) custom-call(s32[1,3]{1,0:T(1,128)S(1)} %add_bitcast_fusion.info_ref, f32[16,1280]{1,0:T(8,128)S(1)} %get-tuple-element.31.begun_ref, bf16[16,2560]{1,0:T(8,128)(2,1)S(1)} %collective-permute-done.6.rest_0_, bf16[16,2560]{1,0:T(8,128)(2,1)S(1)} %collective-permute-done.7.rest_1_, ...), custom_call_target="tpu_custom_call" | custom-call | flops 314572800 | bytes 19660800 | tf_op jit(solution)/shard_map/pallas_call | solution.py:219
  35.1 1.9 %collective-permute-start.10 = (bf16[16,1280]{1,0:T(8,128)(2,1)S(1)}, bf16[16,1280]{1,0:T(8,128)(2,1)S(1)}, u32[]{:S(2)}, u32[]{:S(2)}) collective-permute-start(bf16[16,1280]{1,0:T(8,128)(2,1)S(1)} %convert_element_type.47), channel_id=1, source_target_pairs={{1,0},{3,2},{5,4},{7,6},{9,8},{11,10},{13,12},{15,14},{16,17},{18,... | collective-permute-start | bytes 122888 | tf_op jit(solution)/shard_map/ppermute | solution.py:320
  37.0 0.7 %collective-permute-start.9 = (bf16[16,1280]{1,0:T(8,128)(2,1)S(1)}, bf16[16,1280]{1,0:T(8,128)(2,1)S(1)}, u32[]{:S(2)}, u32[]{:S(2)}) collective-permute-start(bf16[16,1280]{1,0:T(8,128)(2,1)S(1)} %convert_element_type.47), channel_id=1, source_target_pairs={{1,16},{3,18},{5,20},{7,22},{9,24},{11,26},{13,28},{15,30},{16,1},... | collective-permute-start | bytes 122888 | tf_op jit(solution)/shard_map/ppermute | solution.py:320
  37.6 1.0 %collective-permute-done.10 = bf16[16,1280]{1,0:T(8,128)(2,1)S(1)} collective-permute-done((bf16[16,1280]{1,0:T(8,128)(2,1)S(1)}, bf16[16,1280]{1,0:T(8,128)(2,1)S(1)}, u32[]{:S(2)}, u32[]{:S(2)}) %collective-permute-start.10) | collective-permute-done | bytes 40992 | tf_op jit(solution)/shard_map/ppermute | solution.py:320
  38.7 0.0 collective-permute-done.9
  38.7 2.1 %collective-permute-start.11 = (bf16[16,1280]{1,0:T(8,128)(2,1)S(1)}, bf16[16,1280]{1,0:T(8,128)(2,1)S(1)}, u32[]{:S(2)}, u32[]{:S(2)}) collective-permute-start(bf16[16,1280]{1,0:T(8,128)(2,1)S(1)} %add_convert_fusion.1), channel_id=1, source_target_pairs={{0,8},{2,10},{4,12},{6,14},{8,0},{10,2},{12,4},{14,6},{16,24},{18,... | collective-permute-start | bytes 122888 | tf_op jit(solution)/shard_map/ppermute | solution.py:28
  40.8 2.0 %collective-permute-done.11 = bf16[16,1280]{1,0:T(8,128)(2,1)S(1)} collective-permute-done((bf16[16,1280]{1,0:T(8,128)(2,1)S(1)}, bf16[16,1280]{1,0:T(8,128)(2,1)S(1)}, u32[]{:S(2)}, u32[]{:S(2)}) %collective-permute-start.11) | collective-permute-done | bytes 40992 | tf_op jit(solution)/shard_map/ppermute | solution.py:28
  42.8 2.3 %collective-permute-start.14 = (bf16[2,16,1280]{2,1,0:T(8,128)(2,1)S(1)}, bf16[2,16,1280]{2,1,0:T(8,128)(2,1)S(1)}, u32[]{:S(2)}, u32[]{:S(2)}) collective-permute-start(bf16[2,16,1280]{2,1,0:T(8,128)(2,1)S(1)} %pad_maximum_fusion.rest_0_), channel_id=1, source_target_pairs={{0,6},{2,4},{4,2},{6,0},{8,14},{10,12},{12,10},{14,8},{16,22},{18,... | collective-permute-start | bytes 245768 | tf_op jit(solution)/shard_map/ppermute | solution.py:28
  45.1 0.4 collective-permute-start.12
  45.5 0.8 %collective-permute-start.13 = (bf16[2,16,1280]{2,1,0:T(8,128)(2,1)S(1)}, bf16[2,16,1280]{2,1,0:T(8,128)(2,1)S(1)}, u32[]{:S(2)}, u32[]{:S(2)}) collective-permute-start(bf16[2,16,1280]{2,1,0:T(8,128)(2,1)S(1)} %pad_maximum_fusion.rest_0_), channel_id=1, source_target_pairs={{0,2},{2,0},{4,6},{6,4},{8,10},{10,8},{12,14},{14,12},{16,18},{18,... | collective-permute-start | bytes 245768 | tf_op jit(solution)/shard_map/ppermute | solution.py:28
  46.3 1.2 %shard_map.51.rest_1_ = f32[16,768]{1,0:T(8,128)S(1)} custom-call(s32[1,3]{1,0:T(1,128)S(1)} %add_bitcast_fusion.info_ref, bf16[16,768,640]{2,1,0:T(8,128)(2,1)S(1)} %get-tuple-element.24.slots_ref, bf16[2,16,1280]{2,1,0:T(8,128)(2,1)S(1)} %pad_maximum_fusion.rest_0_), custom_call_target="tpu_custom_call" | custom-call | flops 62914560 | bytes 3932160 | tf_op jit(solution)/shard_map/pallas_call | solution.py:270
  47.5 0.7 %collective-permute-done.14.rest_0_ = bf16[2,16,1280]{2,1,0:T(8,128)(2,1)S(1)} collective-permute-done((bf16[2,16,1280]{2,1,0:T(8,128)(2,1)S(1)}, bf16[2,16,1280]{2,1,0:T(8,128)(2,1)S(1)}, u32[]{:S(2)}, u32[]{:S(2)}) %collective-permute-start.14) | collective-permute-done | bytes 81952 | tf_op jit(solution)/shard_map/ppermute | solution.py:28
  48.2 1.2 %shard_map.52.rest_2_ = f32[16,768]{1,0:T(8,128)S(1)} custom-call(s32[1,3]{1,0:T(1,128)S(1)} %add_bitcast_fusion.info_ref, bf16[16,768,640]{2,1,0:T(8,128)(2,1)S(1)} %get-tuple-element.24.slots_ref, bf16[2,16,1280]{2,1,0:T(8,128)(2,1)S(1)} %collective-permute-done.14.rest_0_, f32[16,768]{1,0:T(8,128)S(1)} %shard_map.51.rest_1_), custom_call_target="tpu_custom_call" | custom-call | flops 62914560 | bytes 3932160 | tf_op jit(solution)/shard_map/pallas_call | solution.py:270
  49.3 1.3 %collective-permute-done.12.rest_0_ = bf16[2,16,1280]{2,1,0:T(8,128)(2,1)S(1)} collective-permute-done((bf16[2,16,1280]{2,1,0:T(8,128)(2,1)S(1)}, bf16[2,16,1280]{2,1,0:T(8,128)(2,1)S(1)}, u32[]{:S(2)}, u32[]{:S(2)}) %collective-permute-start.12) | collective-permute-done | bytes 81952 | tf_op jit(solution)/shard_map/ppermute | solution.py:28
  50.6 0.2 collective-permute-done.13.rest_1_
  50.8 2.2 %shard_map.53 = (f32[8,768]{1,0:T(8,128)S(1)}, f32[8,768]{1,0:T(8,128)S(1)}) custom-call(s32[1,3]{1,0:T(1,128)S(1)} %add_bitcast_fusion.info_ref, bf16[16,768,640]{2,1,0:T(8,128)(2,1)S(1)} %get-tuple-element.24.slots_ref, bf16[2,16,1280]{2,1,0:T(8,128)(2,1)S(1)} %collective-permute-done.12.rest_0_, bf16[2,16,1280]{2,1,0:T(8,128)(2,1)S(1)} %collective-permute-done.13.rest_1_, ...), custom_call_target="tpu_custom_call" | custom-call | flops 125829120 | bytes 7864320 | tf_op jit(solution)/shard_map/pallas_call | solution.py:270
  53.0 0.7 %collective-permute-start.15 = (f32[8,768]{1,0:T(8,128)S(1)}, f32[8,768]{1,0:T(8,128)S(1)}, u32[]{:S(2)}, u32[]{:S(2)}) collective-permute-start(f32[8,768]{1,0:T(8,128)S(1)} %get-tuple-element.38), channel_id=1, source_target_pairs={{0,1},{1,0},{2,3},{3,2},{4,5},{5,4},{6,7},{7,6},{8,9},{9,8},{10,11... | collective-permute-start | bytes 73736 | tf_op jit(solution)/shard_map/ppermute | solution.py:28
  53.7 0.8 %collective-permute-done.15 = f32[8,768]{1,0:T(8,128)S(1)} collective-permute-done((f32[8,768]{1,0:T(8,128)S(1)}, f32[8,768]{1,0:T(8,128)S(1)}, u32[]{:S(2)}, u32[]{:S(2)}) %collective-permute-start.15) | collective-permute-done | bytes 24608 | tf_op jit(solution)/shard_map/ppermute | solution.py:28
  54.6 0.6 %select_convert_fusion = bf16[8,768]{1,0:T(8,128)(2,1)} fusion(f32[8,768]{1,0:T(8,128)S(1)} %get-tuple-element.37, f32[8,768]{1,0:T(8,128)S(1)} %collective-permute-done.15, pred[768]{0:T(1024)(128)(4,1)S(1)} %iota_compare_fusion), kind=kLoop, calls=%fused_computation.4 | loop fusion | flops 18432 | bytes 62208 | tf_op jit(solution)/shard_map/convert_element_type | solution.py:357
  (6 shorter events, 0.1 us)
Async XLA Ops:
  5.6 8.9 %collective-permute-start.2 = (bf16[16,2560]{1,0:T(8,128)(2,1)S(1)}, bf16[16,2560]{1,0:T(8,128)(2,1)S(1)}, u32[]{:S(2)}, u32[]{:S(2)}) collective-permute-start(bf16[16,2560]{1,0:T(8,128)(2,1)S(1)} %get-tuple-element.28), channel_id=1, source_target_pairs={{0,2},{2,0},{4,6},{6,4},{8,10},{10,8},{12,14},{14,12},{16,18},{18,... | collective-permute-start | bytes 245768 | tf_op jit(solution)/shard_map/ppermute | solution.py:28
  8.6 5.9 %collective-permute-start.1 = (bf16[16,2560]{1,0:T(8,128)(2,1)S(1)}, bf16[16,2560]{1,0:T(8,128)(2,1)S(1)}, u32[]{:S(2)}, u32[]{:S(2)}) collective-permute-start(bf16[16,2560]{1,0:T(8,128)(2,1)S(1)} %get-tuple-element.27), channel_id=1, source_target_pairs={{0,4},{2,6},{4,0},{6,2},{8,12},{10,14},{12,8},{14,10},{16,20},{18,... | collective-permute-start | bytes 245768 | tf_op jit(solution)/shard_map/ppermute | solution.py:28
  10.1 5.3 %collective-permute-start = (bf16[16,2560]{1,0:T(8,128)(2,1)S(1)}, bf16[16,2560]{1,0:T(8,128)(2,1)S(1)}, u32[]{:S(2)}, u32[]{:S(2)}) collective-permute-start(bf16[16,2560]{1,0:T(8,128)(2,1)S(1)} %get-tuple-element.26), channel_id=1, source_target_pairs={{0,6},{2,4},{4,2},{6,0},{8,14},{10,12},{12,10},{14,8},{16,22},{18,... | collective-permute-start | bytes 245768 | tf_op jit(solution)/shard_map/ppermute | solution.py:28
  15.5 9.3 %collective-permute-start.5 = (bf16[16,2560]{1,0:T(8,128)(2,1)S(1)}, bf16[16,2560]{1,0:T(8,128)(2,1)S(1)}, u32[]{:S(2)}, u32[]{:S(2)}) collective-permute-start(bf16[16,2560]{1,0:T(8,128)(2,1)S(1)} %get-tuple-element.39), channel_id=1, source_target_pairs={{0,24},{2,26},{4,28},{6,30},{8,16},{10,18},{12,20},{14,22},{16,8},... | collective-permute-start | bytes 245768 | tf_op jit(solution)/shard_map/ppermute | solution.py:28
  19.2 5.9 %collective-permute-start.4 = (bf16[16,2560]{1,0:T(8,128)(2,1)S(1)}, bf16[16,2560]{1,0:T(8,128)(2,1)S(1)}, u32[]{:S(2)}, u32[]{:S(2)}) collective-permute-start(bf16[16,2560]{1,0:T(8,128)(2,1)S(1)} %get-tuple-element.39), channel_id=1, source_target_pairs={{0,16},{2,18},{4,20},{6,22},{8,24},{10,26},{12,28},{14,30},{16,0},... | collective-permute-start | bytes 245768 | tf_op jit(solution)/shard_map/ppermute | solution.py:28
  19.2 5.9 %collective-permute-start.3 = (bf16[16,2560]{1,0:T(8,128)(2,1)S(1)}, bf16[16,2560]{1,0:T(8,128)(2,1)S(1)}, u32[]{:S(2)}, u32[]{:S(2)}) collective-permute-start(bf16[16,2560]{1,0:T(8,128)(2,1)S(1)} %get-tuple-element.39), channel_id=1, source_target_pairs={{0,8},{2,10},{4,12},{6,14},{8,0},{10,2},{12,4},{14,6},{16,24},{18,... | collective-permute-start | bytes 245768 | tf_op jit(solution)/shard_map/ppermute | solution.py:28
  25.2 7.2 %collective-permute-start.6 = (bf16[16,2560]{1,0:T(8,128)(2,1)S(1)}, bf16[16,2560]{1,0:T(8,128)(2,1)S(1)}, u32[]{:S(2)}, u32[]{:S(2)}) collective-permute-start(bf16[16,2560]{1,0:T(8,128)(2,1)S(1)} %add_convert_fusion.fitted_ref), channel_id=1, source_target_pairs={{0,6},{2,4},{4,2},{6,0},{8,14},{10,12},{12,10},{14,8},{16,22},{18,... | collective-permute-start | bytes 245768 | tf_op jit(solution)/shard_map/ppermute | solution.py:28
  27.5 4.9 %collective-permute-start.7 = (bf16[16,2560]{1,0:T(8,128)(2,1)S(1)}, bf16[16,2560]{1,0:T(8,128)(2,1)S(1)}, u32[]{:S(2)}, u32[]{:S(2)}) collective-permute-start(bf16[16,2560]{1,0:T(8,128)(2,1)S(1)} %add_convert_fusion.fitted_ref), channel_id=1, source_target_pairs={{0,4},{2,6},{4,0},{6,2},{8,12},{10,14},{12,8},{14,10},{16,20},{18,... | collective-permute-start | bytes 245768 | tf_op jit(solution)/shard_map/ppermute | solution.py:28
  28.0 4.4 %collective-permute-start.8 = (bf16[16,2560]{1,0:T(8,128)(2,1)S(1)}, bf16[16,2560]{1,0:T(8,128)(2,1)S(1)}, u32[]{:S(2)}, u32[]{:S(2)}) collective-permute-start(bf16[16,2560]{1,0:T(8,128)(2,1)S(1)} %add_convert_fusion.fitted_ref), channel_id=1, source_target_pairs={{0,2},{2,0},{4,6},{6,4},{8,10},{10,8},{12,14},{14,12},{16,18},{18,... | collective-permute-start | bytes 245768 | tf_op jit(solution)/shard_map/ppermute | solution.py:28
  35.1 3.6 %collective-permute-start.10 = (bf16[16,1280]{1,0:T(8,128)(2,1)S(1)}, bf16[16,1280]{1,0:T(8,128)(2,1)S(1)}, u32[]{:S(2)}, u32[]{:S(2)}) collective-permute-start(bf16[16,1280]{1,0:T(8,128)(2,1)S(1)} %convert_element_type.47), channel_id=1, source_target_pairs={{1,0},{3,2},{5,4},{7,6},{9,8},{11,10},{13,12},{15,14},{16,17},{18,... | collective-permute-start | bytes 122888 | tf_op jit(solution)/shard_map/ppermute | solution.py:320
  37.0 1.7 %collective-permute-start.9 = (bf16[16,1280]{1,0:T(8,128)(2,1)S(1)}, bf16[16,1280]{1,0:T(8,128)(2,1)S(1)}, u32[]{:S(2)}, u32[]{:S(2)}) collective-permute-start(bf16[16,1280]{1,0:T(8,128)(2,1)S(1)} %convert_element_type.47), channel_id=1, source_target_pairs={{1,16},{3,18},{5,20},{7,22},{9,24},{11,26},{13,28},{15,30},{16,1},... | collective-permute-start | bytes 122888 | tf_op jit(solution)/shard_map/ppermute | solution.py:320
  38.7 4.1 %collective-permute-start.11 = (bf16[16,1280]{1,0:T(8,128)(2,1)S(1)}, bf16[16,1280]{1,0:T(8,128)(2,1)S(1)}, u32[]{:S(2)}, u32[]{:S(2)}) collective-permute-start(bf16[16,1280]{1,0:T(8,128)(2,1)S(1)} %add_convert_fusion.1), channel_id=1, source_target_pairs={{0,8},{2,10},{4,12},{6,14},{8,0},{10,2},{12,4},{14,6},{16,24},{18,... | collective-permute-start | bytes 122888 | tf_op jit(solution)/shard_map/ppermute | solution.py:28
  42.8 5.4 %collective-permute-start.14 = (bf16[2,16,1280]{2,1,0:T(8,128)(2,1)S(1)}, bf16[2,16,1280]{2,1,0:T(8,128)(2,1)S(1)}, u32[]{:S(2)}, u32[]{:S(2)}) collective-permute-start(bf16[2,16,1280]{2,1,0:T(8,128)(2,1)S(1)} %pad_maximum_fusion.rest_0_), channel_id=1, source_target_pairs={{0,6},{2,4},{4,2},{6,0},{8,14},{10,12},{12,10},{14,8},{16,22},{18,... | collective-permute-start | bytes 245768 | tf_op jit(solution)/shard_map/ppermute | solution.py:28
  45.1 5.5 %collective-permute-start.12 = (bf16[2,16,1280]{2,1,0:T(8,128)(2,1)S(1)}, bf16[2,16,1280]{2,1,0:T(8,128)(2,1)S(1)}, u32[]{:S(2)}, u32[]{:S(2)}) collective-permute-start(bf16[2,16,1280]{2,1,0:T(8,128)(2,1)S(1)} %pad_maximum_fusion.rest_0_), channel_id=1, source_target_pairs={{0,4},{2,6},{4,0},{6,2},{8,12},{10,14},{12,8},{14,10},{16,20},{18,... | collective-permute-start | bytes 245768 | tf_op jit(solution)/shard_map/ppermute | solution.py:28
  45.5 5.3 %collective-permute-start.13 = (bf16[2,16,1280]{2,1,0:T(8,128)(2,1)S(1)}, bf16[2,16,1280]{2,1,0:T(8,128)(2,1)S(1)}, u32[]{:S(2)}, u32[]{:S(2)}) collective-permute-start(bf16[2,16,1280]{2,1,0:T(8,128)(2,1)S(1)} %pad_maximum_fusion.rest_0_), channel_id=1, source_target_pairs={{0,2},{2,0},{4,6},{6,4},{8,10},{10,8},{12,14},{14,12},{16,18},{18,... | collective-permute-start | bytes 245768 | tf_op jit(solution)/shard_map/ppermute | solution.py:28
  53.0 1.6 %collective-permute-start.15 = (f32[8,768]{1,0:T(8,128)S(1)}, f32[8,768]{1,0:T(8,128)S(1)}, u32[]{:S(2)}, u32[]{:S(2)}) collective-permute-start(f32[8,768]{1,0:T(8,128)S(1)} %get-tuple-element.38), channel_id=1, source_target_pairs={{0,1},{1,0},{2,3},{3,2},{4,5},{5,4},{6,7},{7,6},{8,9},{9,8},{10,11... | collective-permute-start | bytes 73736 | tf_op jit(solution)/shard_map/ppermute | solution.py:28

commit v5 on v4

--- a/solution.py
+++ b/solution.py
@@ -329,8 +329,9 @@
     if block % step == 0 and len(sizes) == 2:
         arrived = [swap(line_blocks, "pairs", n_pairs, pick) for pick in others]
         (begun,) = back([0], low, info, slots, [line_blocks], split=False)
-        (begun,) = back(others[:1], low, info, slots, arrived[:1], begun, split=False)
-        keep, give = back(others[1:], low, info, slots, arrived[1:], begun)
+        for pick, x in zip(others[:-1], arrived[:-1]):
+            (begun,) = back([pick], low, info, slots, [x], begun, split=False)
+        keep, give = back(others[-1:], low, info, slots, arrived[-1:], begun)
     else:
         mine = me // low
         origin = [((mine ^ i) & 1) * low * block for i in range(2)]

time: 55.3 us -> 55 us (level)
    pallas_call x3 -> x4, Pallas kernels: 4.48 us -> 4.64 us  [back(): pl.pallas_call(functools.partial(back_kernel, which, begun is not None, l...]
  transfers between devices with their start and end apart: 16 -> 16, of which waited for: 8 -> 7; matrix products, arithmetic and copies ran while one was open for 0% -> 0% of each run, Pallas kernels for 27% -> 30%
where the time goes in v5:
time: 55 us; the launch traced here: 54.9 us
  Pallas kernels  24.9 us (45%)
  starting transfers between devices  21.2 us (39%)
  waiting for transfers between devices  7.16 us (13%)
  other arithmetic  0.82 us (1%)
  between operations  0.78 us (1%)
    ppermute x14, starting transfers between devices, swap(): return lax.ppermute(x, axis, [(i, i ^ mask) for i in range(count)])  18.7 us
    ppermute x14, waiting for transfers between devices, swap(): return lax.ppermute(x, axis, [(i, i ^ mask) for i in range(count)])  6.14 us
    pallas_call x1, Pallas kernels, fit_others(): pl.pallas_call(functools.partial(fit_others_kernel, picks, per), out_shap...  4.86 us
    pallas_call x1, Pallas kernels, fetch(): pl.pallas_call(functools.partial(fetch_kernel, picks, top), out_shape=[VM...  4.79 us
    pallas_call x4, Pallas kernels, back(): pl.pallas_call(functools.partial(back_kernel, which, begun is not None, l...  4.64 us
    pallas_call x1, Pallas kernels, fit_own(): pl.pallas_call(functools.partial(fit_own_kernel, per, top), out_shape=[ja...  4.3 us
    pallas_call x1, Pallas kernels, solve_own(): pl.pallas_call(functools.partial(solve_own_kernel, picks, top), out_shape...  3.65 us
    pallas_call x1, Pallas kernels, solve_others(): pl.pallas_call(functools.partial(solve_others_kernel, count, low), out_sh...  2.65 us
  transfers between devices with their start and end apart: 16, of which 7 were waited for; matrix products, arithmetic and copies ran while one was open for 0% of the time, Pallas kernels for 30%

profile of v5, /device:TPU:0, one launch (start us, length us, event | category | flops | bytes accessed | tf_op | source)
XLA Modules:
  0.0 54.9 jit_solution(18055428085681628355)
XLA Ops:
  0.7 0.1 add_bitcast_fusion.info_ref
  0.7 4.9 %shard_map.46 = (bf16[16,2560]{1,0:T(8,128)(2,1)S(1)}, bf16[16,2560]{1,0:T(8,128)(2,1)S(1)}, bf16[16,2560]{1,0:T(8,128)(2,1)S(1)}, bf16[16,768]{1,0:T(8,128)(2,1)S(1)}, bf16[16,768,640]{2,1,0:T(8,128)(2,1)S(1)}) custom-call(s32[1,3]{1,0:T(1,128)S(1)} %add_bitcast_fusion.info_ref, bf16[16,768]{1,0:T(8,128)(2,1)} %dens_hbm.1, bf16[768,10240]{1,0:T(8,128)(2,1)} %tensor_ref.3), custom_call_target="tpu_custom_call" | custom-call | flops 188743680 | bytes 11796480 | tf_op jit(solution)/shard_map/pallas_call | solution.py:100
  5.6 3.0 %collective-permute-start.2 = (bf16[16,2560]{1,0:T(8,128)(2,1)S(1)}, bf16[16,2560]{1,0:T(8,128)(2,1)S(1)}, u32[]{:S(2)}, u32[]{:S(2)}) collective-permute-start(bf16[16,2560]{1,0:T(8,128)(2,1)S(1)} %get-tuple-element.28), channel_id=1, source_target_pairs={{0,2},{2,0},{4,6},{6,4},{8,10},{10,8},{12,14},{14,12},{16,18},{18,... | collective-permute-start | bytes 245768 | tf_op jit(solution)/shard_map/ppermute | solution.py:28
  8.6 1.5 %collective-permute-start.1 = (bf16[16,2560]{1,0:T(8,128)(2,1)S(1)}, bf16[16,2560]{1,0:T(8,128)(2,1)S(1)}, u32[]{:S(2)}, u32[]{:S(2)}) collective-permute-start(bf16[16,2560]{1,0:T(8,128)(2,1)S(1)} %get-tuple-element.27), channel_id=1, source_target_pairs={{0,4},{2,6},{4,0},{6,2},{8,12},{10,14},{12,8},{14,10},{16,20},{18,... | collective-permute-start | bytes 245768 | tf_op jit(solution)/shard_map/ppermute | solution.py:28
  10.1 0.0 collective-permute-start
  10.1 4.3 %shard_map.47 = (f32[16,2560]{1,0:T(8,128)S(1)}, bf16[16,768,640]{2,1,0:T(8,128)(2,1)S(1)}, bf16[2560,1280]{1,0:T(8,128)(2,1)S(1)}) custom-call(s32[1,3]{1,0:T(1,128)S(1)} %add_bitcast_fusion.info_ref, bf16[16,768]{1,0:T(8,128)(2,1)S(1)} %get-tuple-element.22.masked_ref, bf16[768,10240]{1,0:T(8,128)(2,1)} %tensor_ref.3, ...), custom_call_target="tpu_custom_call", output_to_operand_aliasing={{1}: (4, {})} | custom-call | flops 62914560 | bytes 10485760 | tf_op jit(solution)/shard_map/pallas_call | solution.py:142
  14.4 0.0 collective-permute-done.2
  14.5 0.0 collective-permute-done.1
  14.5 1.0 %collective-permute-done = bf16[16,2560]{1,0:T(8,128)(2,1)S(1)} collective-permute-done((bf16[16,2560]{1,0:T(8,128)(2,1)S(1)}, bf16[16,2560]{1,0:T(8,128)(2,1)S(1)}, u32[]{:S(2)}, u32[]{:S(2)}) %collective-permute-start) | collective-permute-done | bytes 81952 | tf_op jit(solution)/shard_map/ppermute | solution.py:28
  15.5 3.7 %collective-permute-start.5 = (bf16[16,2560]{1,0:T(8,128)(2,1)S(1)}, bf16[16,2560]{1,0:T(8,128)(2,1)S(1)}, u32[]{:S(2)}, u32[]{:S(2)}) collective-permute-start(bf16[16,2560]{1,0:T(8,128)(2,1)S(1)} %get-tuple-element.39), channel_id=1, source_target_pairs={{0,24},{2,26},{4,28},{6,30},{8,16},{10,18},{12,20},{14,22},{16,8},... | collective-permute-start | bytes 245768 | tf_op jit(solution)/shard_map/ppermute | solution.py:28
  19.2 0.0 collective-permute-start.4
  19.2 0.8 %collective-permute-start.3 = (bf16[16,2560]{1,0:T(8,128)(2,1)S(1)}, bf16[16,2560]{1,0:T(8,128)(2,1)S(1)}, u32[]{:S(2)}, u32[]{:S(2)}) collective-permute-start(bf16[16,2560]{1,0:T(8,128)(2,1)S(1)} %get-tuple-element.39), channel_id=1, source_target_pairs={{0,8},{2,10},{4,12},{6,14},{8,0},{10,2},{12,4},{14,6},{16,24},{18,... | collective-permute-start | bytes 245768 | tf_op jit(solution)/shard_map/ppermute | solution.py:28
  20.0 4.8 %shard_map.48 = (bf16[2560,1280]{1,0:T(8,128)(2,1)S(1)}, bf16[2560,1280]{1,0:T(8,128)(2,1)S(1)}, f32[16,2560]{1,0:T(8,128)S(1)}) custom-call(s32[1,3]{1,0:T(1,128)S(1)} %add_bitcast_fusion.info_ref, bf16[10240,1280]{1,0:T(8,128)(2,1)} %metric_ref.5, f32[16,2560]{1,0:T(8,128)S(1)} %get-tuple-element.40.own_ref), custom_call_target="tpu_custom_call" | custom-call | bytes 13107200 | tf_op jit(solution)/shard_map/pallas_call | solution.py:168
  24.8 0.0 collective-permute-done.5
  24.8 0.3 collective-permute-done.4
  25.1 0.0 collective-permute-done.3
  25.2 2.4 %collective-permute-start.6 = (bf16[16,2560]{1,0:T(8,128)(2,1)S(1)}, bf16[16,2560]{1,0:T(8,128)(2,1)S(1)}, u32[]{:S(2)}, u32[]{:S(2)}) collective-permute-start(bf16[16,2560]{1,0:T(8,128)(2,1)S(1)} %add_convert_fusion.fitted_ref), channel_id=1, source_target_pairs={{0,6},{2,4},{4,2},{6,0},{8,14},{10,12},{12,10},{14,8},{16,22},{18,... | collective-permute-start | bytes 245768 | tf_op jit(solution)/shard_map/ppermute | solution.py:28
  27.5 0.4 collective-permute-start.7
  28.0 0.8 %collective-permute-start.8 = (bf16[16,2560]{1,0:T(8,128)(2,1)S(1)}, bf16[16,2560]{1,0:T(8,128)(2,1)S(1)}, u32[]{:S(2)}, u32[]{:S(2)}) collective-permute-start(bf16[16,2560]{1,0:T(8,128)(2,1)S(1)} %add_convert_fusion.fitted_ref), channel_id=1, source_target_pairs={{0,2},{2,0},{4,6},{6,4},{8,10},{10,8},{12,14},{14,12},{16,18},{18,... | collective-permute-start | bytes 245768 | tf_op jit(solution)/shard_map/ppermute | solution.py:28
  28.7 3.7 %shard_map.49 = (f32[16,1280]{1,0:T(8,128)S(1)}, bf16[2560,1280]{1,0:T(8,128)(2,1)S(1)}) custom-call(s32[1,3]{1,0:T(1,128)S(1)} %add_bitcast_fusion.info_ref, bf16[10240,1280]{1,0:T(8,128)(2,1)} %metric_ref.5, bf16[16,2560]{1,0:T(8,128)(2,1)S(1)} %add_convert_fusion.fitted_ref, bf16[2560,1280]{1,0:T(8,128)(2,1)S(1)} %get-tuple-element.30.held_ref), custom_call_target="tpu_custom_call" | custom-call | flops 104857600 | bytes 13107200 | tf_op jit(solution)/shard_map/pallas_call | solution.py:193
  32.4 0.0 collective-permute-done.6.rest_0_
  32.4 0.0 collective-permute-done.7.rest_1_
  32.4 0.0 collective-permute-done.8.rest_2_
  32.4 2.7 %shard_map.50 = (f32[16,1280]{1,0:T(8,128)S(1)}, f32[16,1280]{1,0:T(8,128)S(1)}) custom-call(s32[1,3]{1,0:T(1,128)S(1)} %add_bitcast_fusion.info_ref, f32[16,1280]{1,0:T(8,128)S(1)} %get-tuple-element.31.begun_ref, bf16[16,2560]{1,0:T(8,128)(2,1)S(1)} %collective-permute-done.6.rest_0_, bf16[16,2560]{1,0:T(8,128)(2,1)S(1)} %collective-permute-done.7.rest_1_, ...), custom_call_target="tpu_custom_call" | custom-call | flops 314572800 | bytes 19660800 | tf_op jit(solution)/shard_map/pallas_call | solution.py:219
  35.1 1.9 %collective-permute-start.10 = (bf16[16,1280]{1,0:T(8,128)(2,1)S(1)}, bf16[16,1280]{1,0:T(8,128)(2,1)S(1)}, u32[]{:S(2)}, u32[]{:S(2)}) collective-permute-start(bf16[16,1280]{1,0:T(8,128)(2,1)S(1)} %convert_element_type.47), channel_id=1, source_target_pairs={{1,0},{3,2},{5,4},{7,6},{9,8},{11,10},{13,12},{15,14},{16,17},{18,... | collective-permute-start | bytes 122888 | tf_op jit(solution)/shard_map/ppermute | solution.py:320
  37.0 0.7 %collective-permute-start.9 = (bf16[16,1280]{1,0:T(8,128)(2,1)S(1)}, bf16[16,1280]{1,0:T(8,128)(2,1)S(1)}, u32[]{:S(2)}, u32[]{:S(2)}) collective-permute-start(bf16[16,1280]{1,0:T(8,128)(2,1)S(1)} %convert_element_type.47), channel_id=1, source_target_pairs={{1,16},{3,18},{5,20},{7,22},{9,24},{11,26},{13,28},{15,30},{16,1},... | collective-permute-start | bytes 122888 | tf_op jit(solution)/shard_map/ppermute | solution.py:320
  37.6 1.0 %collective-permute-done.10 = bf16[16,1280]{1,0:T(8,128)(2,1)S(1)} collective-permute-done((bf16[16,1280]{1,0:T(8,128)(2,1)S(1)}, bf16[16,1280]{1,0:T(8,128)(2,1)S(1)}, u32[]{:S(2)}, u32[]{:S(2)}) %collective-permute-start.10) | collective-permute-done | bytes 40992 | tf_op jit(solution)/shard_map/ppermute | solution.py:320
  38.7 0.0 collective-permute-done.9
  38.7 2.1 %collective-permute-start.11 = (bf16[16,1280]{1,0:T(8,128)(2,1)S(1)}, bf16[16,1280]{1,0:T(8,128)(2,1)S(1)}, u32[]{:S(2)}, u32[]{:S(2)}) collective-permute-start(bf16[16,1280]{1,0:T(8,128)(2,1)S(1)} %add_convert_fusion.1), channel_id=1, source_target_pairs={{0,8},{2,10},{4,12},{6,14},{8,0},{10,2},{12,4},{14,6},{16,24},{18,... | collective-permute-start | bytes 122888 | tf_op jit(solution)/shard_map/ppermute | solution.py:28
  40.8 2.0 %collective-permute-done.11 = bf16[16,1280]{1,0:T(8,128)(2,1)S(1)} collective-permute-done((bf16[16,1280]{1,0:T(8,128)(2,1)S(1)}, bf16[16,1280]{1,0:T(8,128)(2,1)S(1)}, u32[]{:S(2)}, u32[]{:S(2)}) %collective-permute-start.11) | collective-permute-done | bytes 40992 | tf_op jit(solution)/shard_map/ppermute | solution.py:28
  42.8 2.3 %collective-permute-start.14 = (bf16[2,16,1280]{2,1,0:T(8,128)(2,1)S(1)}, bf16[2,16,1280]{2,1,0:T(8,128)(2,1)S(1)}, u32[]{:S(2)}, u32[]{:S(2)}) collective-permute-start(bf16[2,16,1280]{2,1,0:T(8,128)(2,1)S(1)} %pad_maximum_fusion.rest_0_), channel_id=1, source_target_pairs={{0,6},{2,4},{4,2},{6,0},{8,14},{10,12},{12,10},{14,8},{16,22},{18,... | collective-permute-start | bytes 245768 | tf_op jit(solution)/shard_map/ppermute | solution.py:28
  45.1 0.4 collective-permute-start.13
  45.5 0.8 %collective-permute-start.12 = (bf16[2,16,1280]{2,1,0:T(8,128)(2,1)S(1)}, bf16[2,16,1280]{2,1,0:T(8,128)(2,1)S(1)}, u32[]{:S(2)}, u32[]{:S(2)}) collective-permute-start(bf16[2,16,1280]{2,1,0:T(8,128)(2,1)S(1)} %pad_maximum_fusion.rest_0_), channel_id=1, source_target_pairs={{0,2},{2,0},{4,6},{6,4},{8,10},{10,8},{12,14},{14,12},{16,18},{18,... | collective-permute-start | bytes 245768 | tf_op jit(solution)/shard_map/ppermute | solution.py:28
  46.3 1.2 %shard_map.51.rest_1_ = f32[16,768]{1,0:T(8,128)S(1)} custom-call(s32[1,3]{1,0:T(1,128)S(1)} %add_bitcast_fusion.info_ref, bf16[16,768,640]{2,1,0:T(8,128)(2,1)S(1)} %get-tuple-element.24.slots_ref, bf16[2,16,1280]{2,1,0:T(8,128)(2,1)S(1)} %pad_maximum_fusion.rest_0_), custom_call_target="tpu_custom_call" | custom-call | flops 62914560 | bytes 3932160 | tf_op jit(solution)/shard_map/pallas_call | solution.py:270
  47.5 0.7 %collective-permute-done.14.rest_0_ = bf16[2,16,1280]{2,1,0:T(8,128)(2,1)S(1)} collective-permute-done((bf16[2,16,1280]{2,1,0:T(8,128)(2,1)S(1)}, bf16[2,16,1280]{2,1,0:T(8,128)(2,1)S(1)}, u32[]{:S(2)}, u32[]{:S(2)}) %collective-permute-start.14) | collective-permute-done | bytes 81952 | tf_op jit(solution)/shard_map/ppermute | solution.py:28
  48.2 1.2 %shard_map.52.rest_1_ = f32[16,768]{1,0:T(8,128)S(1)} custom-call(s32[1,3]{1,0:T(1,128)S(1)} %add_bitcast_fusion.info_ref, bf16[16,768,640]{2,1,0:T(8,128)(2,1)S(1)} %get-tuple-element.24.slots_ref, bf16[2,16,1280]{2,1,0:T(8,128)(2,1)S(1)} %collective-permute-done.14.rest_0_, f32[16,768]{1,0:T(8,128)S(1)} %shard_map.51.rest_1_), custom_call_target="tpu_custom_call" | custom-call | flops 62914560 | bytes 3932160 | tf_op jit(solution)/shard_map/pallas_call | solution.py:270
  49.3 1.3 %collective-permute-done.13.rest_0_ = bf16[2,16,1280]{2,1,0:T(8,128)(2,1)S(1)} collective-permute-done((bf16[2,16,1280]{2,1,0:T(8,128)(2,1)S(1)}, bf16[2,16,1280]{2,1,0:T(8,128)(2,1)S(1)}, u32[]{:S(2)}, u32[]{:S(2)}) %collective-permute-start.13) | collective-permute-done | bytes 81952 | tf_op jit(solution)/shard_map/ppermute | solution.py:28
  50.6 1.2 %shard_map.53.rest_1_ = f32[16,768]{1,0:T(8,128)S(1)} custom-call(s32[1,3]{1,0:T(1,128)S(1)} %add_bitcast_fusion.info_ref, bf16[16,768,640]{2,1,0:T(8,128)(2,1)S(1)} %get-tuple-element.24.slots_ref, bf16[2,16,1280]{2,1,0:T(8,128)(2,1)S(1)} %collective-permute-done.13.rest_0_, f32[16,768]{1,0:T(8,128)S(1)} %shard_map.52.rest_1_), custom_call_target="tpu_custom_call" | custom-call | flops 62914560 | bytes 3932160 | tf_op jit(solution)/shard_map/pallas_call | solution.py:270
  51.7 0.0 collective-permute-done.12.rest_0_
  51.7 1.2 %shard_map.54 = (f32[8,768]{1,0:T(8,128)S(1)}, f32[8,768]{1,0:T(8,128)S(1)}) custom-call(s32[1,3]{1,0:T(1,128)S(1)} %add_bitcast_fusion.info_ref, bf16[16,768,640]{2,1,0:T(8,128)(2,1)S(1)} %get-tuple-element.24.slots_ref, bf16[2,16,1280]{2,1,0:T(8,128)(2,1)S(1)} %collective-permute-done.12.rest_0_, f32[16,768]{1,0:T(8,128)S(1)} %shard_map.53.rest_1_), custom_call_target="tpu_custom_call" | custom-call | flops 62914560 | bytes 3932160 | tf_op jit(solution)/shard_map/pallas_call | solution.py:270
  52.9 0.5 collective-permute-start.15
  53.4 0.8 %collective-permute-done.15 = f32[8,768]{1,0:T(8,128)S(1)} collective-permute-done((f32[8,768]{1,0:T(8,128)S(1)}, f32[8,768]{1,0:T(8,128)S(1)}, u32[]{:S(2)}, u32[]{:S(2)}) %collective-permute-start.15) | collective-permute-done | bytes 24608 | tf_op jit(solution)/shard_map/ppermute | solution.py:28
  54.3 0.6 %select_convert_fusion = bf16[8,768]{1,0:T(8,128)(2,1)} fusion(f32[8,768]{1,0:T(8,128)S(1)} %get-tuple-element.37, f32[8,768]{1,0:T(8,128)S(1)} %collective-permute-done.15, pred[768]{0:T(1024)(128)(4,1)S(1)} %iota_compare_fusion), kind=kLoop, calls=%fused_computation.4 | loop fusion | flops 18432 | bytes 62208 | tf_op jit(solution)/shard_map/convert_element_type | solution.py:358
  (6 shorter events, 0.1 us)
Async XLA Ops:
  5.6 8.9 %collective-permute-start.2 = (bf16[16,2560]{1,0:T(8,128)(2,1)S(1)}, bf16[16,2560]{1,0:T(8,128)(2,1)S(1)}, u32[]{:S(2)}, u32[]{:S(2)}) collective-permute-start(bf16[16,2560]{1,0:T(8,128)(2,1)S(1)} %get-tuple-element.28), channel_id=1, source_target_pairs={{0,2},{2,0},{4,6},{6,4},{8,10},{10,8},{12,14},{14,12},{16,18},{18,... | collective-permute-start | bytes 245768 | tf_op jit(solution)/shard_map/ppermute | solution.py:28
  8.6 5.9 %collective-permute-start.1 = (bf16[16,2560]{1,0:T(8,128)(2,1)S(1)}, bf16[16,2560]{1,0:T(8,128)(2,1)S(1)}, u32[]{:S(2)}, u32[]{:S(2)}) collective-permute-start(bf16[16,2560]{1,0:T(8,128)(2,1)S(1)} %get-tuple-element.27), channel_id=1, source_target_pairs={{0,4},{2,6},{4,0},{6,2},{8,12},{10,14},{12,8},{14,10},{16,20},{18,... | collective-permute-start | bytes 245768 | tf_op jit(solution)/shard_map/ppermute | solution.py:28
  10.1 5.3 %collective-permute-start = (bf16[16,2560]{1,0:T(8,128)(2,1)S(1)}, bf16[16,2560]{1,0:T(8,128)(2,1)S(1)}, u32[]{:S(2)}, u32[]{:S(2)}) collective-permute-start(bf16[16,2560]{1,0:T(8,128)(2,1)S(1)} %get-tuple-element.26), channel_id=1, source_target_pairs={{0,6},{2,4},{4,2},{6,0},{8,14},{10,12},{12,10},{14,8},{16,22},{18,... | collective-permute-start | bytes 245768 | tf_op jit(solution)/shard_map/ppermute | solution.py:28
  15.5 9.3 %collective-permute-start.5 = (bf16[16,2560]{1,0:T(8,128)(2,1)S(1)}, bf16[16,2560]{1,0:T(8,128)(2,1)S(1)}, u32[]{:S(2)}, u32[]{:S(2)}) collective-permute-start(bf16[16,2560]{1,0:T(8,128)(2,1)S(1)} %get-tuple-element.39), channel_id=1, source_target_pairs={{0,24},{2,26},{4,28},{6,30},{8,16},{10,18},{12,20},{14,22},{16,8},... | collective-permute-start | bytes 245768 | tf_op jit(solution)/shard_map/ppermute | solution.py:28
  19.2 5.9 %collective-permute-start.4 = (bf16[16,2560]{1,0:T(8,128)(2,1)S(1)}, bf16[16,2560]{1,0:T(8,128)(2,1)S(1)}, u32[]{:S(2)}, u32[]{:S(2)}) collective-permute-start(bf16[16,2560]{1,0:T(8,128)(2,1)S(1)} %get-tuple-element.39), channel_id=1, source_target_pairs={{0,16},{2,18},{4,20},{6,22},{8,24},{10,26},{12,28},{14,30},{16,0},... | collective-permute-start | bytes 245768 | tf_op jit(solution)/shard_map/ppermute | solution.py:28
  19.2 5.9 %collective-permute-start.3 = (bf16[16,2560]{1,0:T(8,128)(2,1)S(1)}, bf16[16,2560]{1,0:T(8,128)(2,1)S(1)}, u32[]{:S(2)}, u32[]{:S(2)}) collective-permute-start(bf16[16,2560]{1,0:T(8,128)(2,1)S(1)} %get-tuple-element.39), channel_id=1, source_target_pairs={{0,8},{2,10},{4,12},{6,14},{8,0},{10,2},{12,4},{14,6},{16,24},{18,... | collective-permute-start | bytes 245768 | tf_op jit(solution)/shard_map/ppermute | solution.py:28
  25.2 7.2 %collective-permute-start.6 = (bf16[16,2560]{1,0:T(8,128)(2,1)S(1)}, bf16[16,2560]{1,0:T(8,128)(2,1)S(1)}, u32[]{:S(2)}, u32[]{:S(2)}) collective-permute-start(bf16[16,2560]{1,0:T(8,128)(2,1)S(1)} %add_convert_fusion.fitted_ref), channel_id=1, source_target_pairs={{0,6},{2,4},{4,2},{6,0},{8,14},{10,12},{12,10},{14,8},{16,22},{18,... | collective-permute-start | bytes 245768 | tf_op jit(solution)/shard_map/ppermute | solution.py:28
  27.5 4.9 %collective-permute-start.7 = (bf16[16,2560]{1,0:T(8,128)(2,1)S(1)}, bf16[16,2560]{1,0:T(8,128)(2,1)S(1)}, u32[]{:S(2)}, u32[]{:S(2)}) collective-permute-start(bf16[16,2560]{1,0:T(8,128)(2,1)S(1)} %add_convert_fusion.fitted_ref), channel_id=1, source_target_pairs={{0,4},{2,6},{4,0},{6,2},{8,12},{10,14},{12,8},{14,10},{16,20},{18,... | collective-permute-start | bytes 245768 | tf_op jit(solution)/shard_map/ppermute | solution.py:28
  28.0 4.4 %collective-permute-start.8 = (bf16[16,2560]{1,0:T(8,128)(2,1)S(1)}, bf16[16,2560]{1,0:T(8,128)(2,1)S(1)}, u32[]{:S(2)}, u32[]{:S(2)}) collective-permute-start(bf16[16,2560]{1,0:T(8,128)(2,1)S(1)} %add_convert_fusion.fitted_ref), channel_id=1, source_target_pairs={{0,2},{2,0},{4,6},{6,4},{8,10},{10,8},{12,14},{14,12},{16,18},{18,... | collective-permute-start | bytes 245768 | tf_op jit(solution)/shard_map/ppermute | solution.py:28
  35.1 3.6 %collective-permute-start.10 = (bf16[16,1280]{1,0:T(8,128)(2,1)S(1)}, bf16[16,1280]{1,0:T(8,128)(2,1)S(1)}, u32[]{:S(2)}, u32[]{:S(2)}) collective-permute-start(bf16[16,1280]{1,0:T(8,128)(2,1)S(1)} %convert_element_type.47), channel_id=1, source_target_pairs={{1,0},{3,2},{5,4},{7,6},{9,8},{11,10},{13,12},{15,14},{16,17},{18,... | collective-permute-start | bytes 122888 | tf_op jit(solution)/shard_map/ppermute | solution.py:320
  37.0 1.7 %collective-permute-start.9 = (bf16[16,1280]{1,0:T(8,128)(2,1)S(1)}, bf16[16,1280]{1,0:T(8,128)(2,1)S(1)}, u32[]{:S(2)}, u32[]{:S(2)}) collective-permute-start(bf16[16,1280]{1,0:T(8,128)(2,1)S(1)} %convert_element_type.47), channel_id=1, source_target_pairs={{1,16},{3,18},{5,20},{7,22},{9,24},{11,26},{13,28},{15,30},{16,1},... | collective-permute-start | bytes 122888 | tf_op jit(solution)/shard_map/ppermute | solution.py:320
  38.7 4.1 %collective-permute-start.11 = (bf16[16,1280]{1,0:T(8,128)(2,1)S(1)}, bf16[16,1280]{1,0:T(8,128)(2,1)S(1)}, u32[]{:S(2)}, u32[]{:S(2)}) collective-permute-start(bf16[16,1280]{1,0:T(8,128)(2,1)S(1)} %add_convert_fusion.1), channel_id=1, source_target_pairs={{0,8},{2,10},{4,12},{6,14},{8,0},{10,2},{12,4},{14,6},{16,24},{18,... | collective-permute-start | bytes 122888 | tf_op jit(solution)/shard_map/ppermute | solution.py:28
  42.8 5.4 %collective-permute-start.14 = (bf16[2,16,1280]{2,1,0:T(8,128)(2,1)S(1)}, bf16[2,16,1280]{2,1,0:T(8,128)(2,1)S(1)}, u32[]{:S(2)}, u32[]{:S(2)}) collective-permute-start(bf16[2,16,1280]{2,1,0:T(8,128)(2,1)S(1)} %pad_maximum_fusion.rest_0_), channel_id=1, source_target_pairs={{0,6},{2,4},{4,2},{6,0},{8,14},{10,12},{12,10},{14,8},{16,22},{18,... | collective-permute-start | bytes 245768 | tf_op jit(solution)/shard_map/ppermute | solution.py:28
  45.1 5.5 %collective-permute-start.13 = (bf16[2,16,1280]{2,1,0:T(8,128)(2,1)S(1)}, bf16[2,16,1280]{2,1,0:T(8,128)(2,1)S(1)}, u32[]{:S(2)}, u32[]{:S(2)}) collective-permute-start(bf16[2,16,1280]{2,1,0:T(8,128)(2,1)S(1)} %pad_maximum_fusion.rest_0_), channel_id=1, source_target_pairs={{0,4},{2,6},{4,0},{6,2},{8,12},{10,14},{12,8},{14,10},{16,20},{18,... | collective-permute-start | bytes 245768 | tf_op jit(solution)/shard_map/ppermute | solution.py:28
  45.5 6.2 %collective-permute-start.12 = (bf16[2,16,1280]{2,1,0:T(8,128)(2,1)S(1)}, bf16[2,16,1280]{2,1,0:T(8,128)(2,1)S(1)}, u32[]{:S(2)}, u32[]{:S(2)}) collective-permute-start(bf16[2,16,1280]{2,1,0:T(8,128)(2,1)S(1)} %pad_maximum_fusion.rest_0_), channel_id=1, source_target_pairs={{0,2},{2,0},{4,6},{6,4},{8,10},{10,8},{12,14},{14,12},{16,18},{18,... | collective-permute-start | bytes 245768 | tf_op jit(solution)/shard_map/ppermute | solution.py:28
  52.9 1.3 %collective-permute-start.15 = (f32[8,768]{1,0:T(8,128)S(1)}, f32[8,768]{1,0:T(8,128)S(1)}, u32[]{:S(2)}, u32[]{:S(2)}) collective-permute-start(f32[8,768]{1,0:T(8,128)S(1)} %get-tuple-element.38), channel_id=1, source_target_pairs={{0,1},{1,0},{2,3},{3,2},{4,5},{5,4},{6,7},{7,6},{8,9},{9,8},{10,11... | collective-permute-start | bytes 73736 | tf_op jit(solution)/shard_map/ppermute | solution.py:28
